TPU v7x, 256 devices: a whole 4x4x8 slice. The times are simulated.
256 devices in a mesh: row: 64 (over z, x_lo, y), col: 4 (over x_hi, core).
Axes of the slice: x: 4 (x_hi: 2, x_lo: 2; x = x_hi * 2 + x_lo), y: 4, z: 8, core: 2. Of those that a mesh axis runs over, the one named last changes fastest.
Arguments:
- factor_rows: float32 [2, 1024, 131072], P(None, 'col', 'row'), may hold values from -0.015625 to 0.015625
- solved_rows: float32 [131072, 512], P('row'), may hold values from -16 to 16
- right_side: float32 [2, 1024, 512], P(None, 'col', 'row'), may hold values from -6 to 6
- inverse: float32 [2, 1024, 1024], P(None, 'col'), may hold values from -1 to 2, as said below
- coupling: float32 [1024, 1024], P('col'), may hold values from -0.1875 to 0.1875
Outputs:
- forward: float32 [2, 1024, 512], P(None, 'col', 'row')
- backward: float32 [2, 1024, 512], P(None, 'col', 'row')
Inputs may be any that keep to these rules, and one draw needn't show every extreme that they name: Each block of inverse is lower triangular with a positive diagonal.
All inputs are finite; a program needn't handle non-finite values.
Results may differ from a plain program's by a relative error of at most 0.00013.
Values sent between devices are 32-bit elements; how exact they have to be, the bound alone decides.
No kernel may reach another device: no remote copies, remote signals or barrier semaphores. Data moves between devices by JAX's collectives and lax.ppermute only.
A program may use at most 128 MiB of HBM per device.

v0:
```python
import jax
import jax.numpy as jnp
from jax import lax
from jax.sharding import PartitionSpec as P


def matmul(left, right):
    return jnp.dot(left, right, preferred_element_type=jnp.float32, precision=lax.Precision.HIGHEST)


def shards(factor_rows, solved_rows, right_side, inverse, coupling):
    quarter = inverse.shape[1]
    total_rhs = solved_rows.shape[1]
    local_rhs = total_rhs // lax.axis_size("row")
    flat = factor_rows.reshape(2 * quarter, factor_rows.shape[2])
    reduced = lax.psum_scatter(
        lax.dot_general(
            solved_rows,
            flat,
            (((0,), (1,)), ((), ())),
            preferred_element_type=jnp.float32,
            precision=lax.Precision.HIGHEST,
        ),
        "row",
        scatter_dimension=0,
        tiled=True,
    )
    update = reduced.T.reshape(2, quarter, local_rhs)
    residual_part = right_side - update
    gathered = lax.all_gather(residual_part[0], "col", axis=0, tiled=True)
    first_forward = matmul(inverse[0], gathered)
    first_whole = lax.all_gather(first_forward, "col", axis=0, tiled=True)
    second_part = residual_part[1] - matmul(coupling, first_whole)
    second_whole = lax.all_gather(second_part, "col", axis=0, tiled=True)
    second_forward = matmul(inverse[1], second_whole)
    second_backward = lax.psum_scatter(
        matmul(inverse[1].T, second_forward), "col", scatter_dimension=0, tiled=True
    )
    carried = lax.psum_scatter(
        matmul(coupling.T, second_backward), "col", scatter_dimension=0, tiled=True
    )
    first_backward = lax.psum_scatter(
        matmul(inverse[0].T, first_forward - carried), "col", scatter_dimension=0, tiled=True
    )
    forward = jnp.stack([first_forward, second_forward])
    backward = jnp.stack([first_backward, second_backward])
    return (forward, backward)


def solution(mesh):
    placed = (
        P(None, "col", "row"),
        P("row", None),
        P(None, "col", "row"),
        P(None, "col", None),
        P("col", None),
    )
    return jax.shard_map(
        shards,
        mesh=mesh,
        in_specs=placed,
        out_specs=(P(None, "col", "row"), P(None, "col", "row")),
        check_vma=False,
    )
```

profile of v0, /device:TPU:1, one launch (start us, length us, event | category | flops | bytes accessed | tf_op | source)
XLA Modules:
  0.0 470.3 jit_solution(17397169601459535568)
XLA Ops:
  7.2 0.0 copy-start
  7.2 0.0 reduce-scatter.5.cloned.1.call-start
  7.2 0.0 copy-start.3
  7.2 0.0 copy-start.1
  7.2 16.8 %fusion.14 = f32[512,512]{1,0:T(8,128)} fusion(f32[2048,512]{1,0:T(8,128)} %param.6, f32[512,2048]{1,0:T(8,128)} %bitcast.51), kind=kOutput, calls=%fused_computation.21 | convolution fusion | flops 6442450944 | bytes 9437184 | tf_op jit(solution)/shard_map/dot_general | solution.py:17
  24.0 0.0 reduce-scatter.5.cloned.1.call-update
  24.0 0.0 reduce-scatter.7.cloned.1.call-start
  24.1 267.3 %reduce-scatter.5.cloned.1.call-done = f32[8,512]{1,0:T(8,128)} async-done(((f32[512,512]{1,0:T(8,128)}), f32[8,512]{1,0:T(8,128)}) %reduce-scatter.5.cloned.1.call-update) | async-done | bytes 16400 | tf_op jit(solution)/shard_map/reduce_scatter | solution.py:16
  291.4 0.0 copy-done.3
  291.4 0.7 sub.9
  292.1 59.5 %all-gather = f32[1,1024,8]{1,2,0:T(8,128)S(1)} all-gather(f32[1,256,8]{1,2,0:T(8,128)S(1)} %slice.18), channel_id=2, replica_groups=mesh['row'=64,'col'=4] {'col'}, dimensions={1}, use_global_device_ids=true | all-gather | bytes 40960 | tf_op jit(solution)/shard_map/all_gather | solution.py:30
  351.6 0.0 copy-done.1
  351.6 0.9 fusion.5
  352.5 6.7 %all_gather.10 = f32[1024,8]{0,1:T(8,128)S(1)} all-gather(f32[256,8]{0,1:T(8,128)S(1)} %bitcast.52), channel_id=1, replica_groups=mesh['row'=64,'col'=4] {'col'}, dimensions={0}, use_global_device_ids=true | all-gather | bytes 40960 | tf_op jit(solution)/shard_map/all_gather | solution.py:32
  359.2 0.0 copy-done
  359.2 0.9 fusion
  360.1 6.7 %all_gather.11 = f32[1024,8]{0,1:T(8,128)S(1)} all-gather(f32[256,8]{0,1:T(8,128)S(1)} %fusion), channel_id=1, replica_groups=mesh['row'=64,'col'=4] {'col'}, dimensions={0}, use_global_device_ids=true | all-gather | bytes 40960 | tf_op jit(solution)/shard_map/all_gather | solution.py:34
  366.8 0.9 fusion.2
  367.8 1.2 convolution_bitcast_fusion.2
  369.0 0.0 reduce-scatter.7.cloned.1.call-update
  369.0 0.0 reduce-scatter.9.cloned.1.call-start
  369.1 26.2 %reduce-scatter.7.cloned.1.call-done = f32[256,8]{0,1:T(8,128)} async-done(((f32[1024,8]{0,1:T(8,128)}), f32[256,8]{0,1:T(8,128)}) %reduce-scatter.7.cloned.1.call-update) | async-done | bytes 8208 | tf_op jit(solution)/shard_map/reduce_scatter | solution.py:36
  395.3 0.0 copy-start.2
  395.3 2.0 convolution_bitcast_fusion.1
  397.3 0.0 reduce-scatter.9.cloned.1.call-update
  397.3 0.0 reduce-scatter.11.cloned.1.call-start
  397.3 31.5 %reduce-scatter.9.cloned.1.call-done = f32[256,8]{0,1:T(8,128)} async-done(((f32[1024,8]{0,1:T(8,128)}), f32[256,8]{0,1:T(8,128)}) %reduce-scatter.9.cloned.1.call-update) | async-done | bytes 8208 | tf_op jit(solution)/shard_map/reduce_scatter | solution.py:39
  428.8 1.9 convolution_bitcast_fusion
  430.7 0.0 reduce-scatter.11.cloned.1.call-update
  430.7 0.6 pad_maximum_fusion
  431.3 31.1 %reduce-scatter.11.cloned.1.call-done = f32[256,8]{0,1:T(8,128)} async-done(((f32[1024,8]{0,1:T(8,128)}), f32[256,8]{0,1:T(8,128)}) %reduce-scatter.11.cloned.1.call-update) | async-done | bytes 8208 | tf_op jit(solution)/shard_map/reduce_scatter | solution.py:42
  462.4 0.0 copy-done.2
  462.4 1.3 pad_maximum_fusion.1
  (1 shorter events, 0.0 us)
Async XLA Ops:
  7.2 352.1 %copy-start = (f32[256,1024]{1,0:T(8,128)S(1)}, f32[256,1024]{1,0:T(8,128)}, u32[]{:S(2)}) copy-start(f32[256,1024]{1,0:T(8,128)} %param.9) | copy-start | bytes 3145732
  7.2 284.2 %reduce-scatter.5.cloned.1.call-start = ((), (), s32[]{:S(2)}) async-start(), calls=%async_computation.4 | async-start | bytes 1064960 | tf_op jit(solution)/shard_map/reduce_scatter | solution.py:16
  7.2 284.2 %copy-start.3 = (f32[2,256,8]{1,2,0:T(8,128)S(1)}, f32[2,256,8]{1,2,0:T(8,128)}, u32[]{:S(2)}) copy-start(f32[2,256,8]{1,2,0:T(8,128)} %param.7) | copy-start | bytes 49156
  7.2 344.4 %copy-start.1 = (f32[2,256,1024]{2,1,0:T(8,128)S(1)}, f32[2,256,1024]{2,1,0:T(8,128)}, u32[]{:S(2)}) copy-start(f32[2,256,1024]{2,1,0:T(8,128)} %param.8) | copy-start | bytes 6291460
  24.0 371.2 %reduce-scatter.7.cloned.1.call-start = ((), (), s32[]{:S(2)}) async-start(), calls=%async_computation.5 | async-start | bytes 40960 | tf_op jit(solution)/shard_map/reduce_scatter | solution.py:36
  369.0 59.8 %reduce-scatter.9.cloned.1.call-start = ((), (), s32[]{:S(2)}) async-start(), calls=%async_computation.6 | async-start | bytes 40960 | tf_op jit(solution)/shard_map/reduce_scatter | solution.py:39
  395.3 67.2 %copy-start.2 = (f32[256,8]{0,1:T(8,128)S(1)}, f32[256,8]{0,1:T(8,128)}, u32[]{:S(2)}) copy-start(f32[256,8]{0,1:T(8,128)} %reduce-scatter.7.cloned.1.call-done) | copy-start | bytes 24580
  397.3 65.1 %reduce-scatter.11.cloned.1.call-start = ((), (), s32[]{:S(2)}) async-start(), calls=%async_computation.7 | async-start | bytes 40960 | tf_op jit(solution)/shard_map/reduce_scatter | solution.py:42
Sparse Core Ops, SparseCore 0:
  24.2 267.1 reduce-scatter.4
  369.1 26.0 reduce-scatter.6
  397.9 30.8 reduce-scatter.8
  431.5 30.8 reduce-scatter.10
where the time goes:
time: 471 us; the launch traced here: 470 us
  waiting for transfers between devices  356 us (76%)
  blocking collectives  72.9 us (15%)
  matrix products  24.6 us (5%)
  between operations  13.8 us (3%)
    reduce_scatter x1, waiting for transfers between devices, shards(): lax.psum_scatter(lax.dot_general(solved_rows, flat, (((0,), (1,)), ((), (...  267 us
    all_gather x1, blocking collectives, shards(): gathered = lax.all_gather(residual_part[0], 'col', axis=0, tiled=True)  59.5 us
    reduce_scatter x1, waiting for transfers between devices, shards(): lax.psum_scatter(matmul(coupling.T, second_backward), 'col', scatter_dime...  31.5 us
    reduce_scatter x1, waiting for transfers between devices, shards(): lax.psum_scatter(matmul(inverse[0].T, first_forward - carried), 'col', sc...  31.1 us
    reduce_scatter x1, waiting for transfers between devices, shards(): lax.psum_scatter(matmul(inverse[1].T, second_forward), 'col', scatter_dim...  26.2 us
    dot_general x1, matrix products, shards(): lax.dot_general(solved_rows, flat, (((0,), (1,)), ((), ())), preferred_el...  16.8 us
  transfers between devices with their start and end apart: 4, of which 4 were waited for; matrix products, arithmetic and copies ran while one was open for 0% of the time, Pallas kernels for 0%

commit v1 on v0

v1 whole, which is shorter than its diff:
```python
import jax
import jax.numpy as jnp
from jax import lax
from jax.sharding import Mesh, PartitionSpec as P

AXES = ("z", "xl", "y", "xh", "core")
ROW = ("z", "xl", "y")
COL = ("xh", "core")


def dot(left, right, dims):
    return lax.dot_general(
        left, right, (dims, ((), ())), preferred_element_type=jnp.float32, precision=lax.Precision.HIGHEST
    )


def from_partner(block, flip):
    return lax.ppermute(block, COL, [(s, s ^ flip) for s in range(4)])


def in_order(pieces, mine):
    high, low = mine // 2, mine % 2
    a = [jnp.where(low == 1, pieces[k ^ 1], pieces[k]) for k in range(4)]
    return [jnp.where(high == 1, a[k ^ 2], a[k]) for k in range(4)]


def gather(block):
    return [block] + [from_partner(block, k) for k in (1, 2, 3)]


def total(block):
    g = gather(block)
    return (g[0] + g[1]) + (g[2] + g[3])


def block_of(array, index, axis):
    return lax.dynamic_slice_in_dim(array, index * 256, 256, axis)


def shards(factor_rows, solved_rows, right_side, inverse, coupling):
    mine = lax.axis_index(COL)
    flat = factor_rows.reshape(512, 2048)
    columns = in_order(
        [block_of(coupling, mine, 1)] + [from_partner(block_of(coupling, mine ^ k, 1), k) for k in (1, 2, 3)], mine
    )
    columns = jnp.concatenate(columns, axis=0)
    part = lax.dot_general(
        solved_rows, flat, (((0,), (1,)), ((), ())), preferred_element_type=jnp.float32, precision=lax.Precision.HIGH
    )
    part = part.reshape(8, 8, 8, 512).transpose(1, 0, 2, 3).reshape(8, 64, 512)
    part = lax.all_to_all(part, ("xl", "y"), 0, 0, tiled=True).sum(0)
    part = lax.all_to_all(part.reshape(8, 8, 512), "z", 0, 0, tiled=True).sum(0)
    right = right_side.transpose(0, 2, 1)
    r0 = right[0] - part[:, :256]
    r1 = right[1] - part[:, 256:]
    r0_whole = jnp.concatenate(in_order(gather(r0), mine), axis=1)
    f0 = dot(r0_whole, inverse[0], ((1,), (1,)))
    s_part = -dot(f0, columns, ((1,), (1,)))
    s_part = s_part + jnp.concatenate([jnp.where(mine == k, r1, 0.0) for k in range(4)], axis=1)
    f1 = dot(total(s_part), inverse[1], ((1,), (1,)))
    b1 = total(dot(f1, inverse[1], ((1,), (0,))))
    g = f0 - dot(b1, columns, ((1,), (0,)))
    b0_part = dot(g, inverse[0], ((1,), (0,)))
    got = [block_of(b0_part, mine, 1)] + [from_partner(block_of(b0_part, mine ^ k, 1), k) for k in (1, 2, 3)]
    b0 = (got[0] + got[1]) + (got[2] + got[3])
    forward = jnp.stack([f0, f1]).transpose(0, 2, 1)
    backward = jnp.stack([b0, block_of(b1, mine, 1)]).transpose(0, 2, 1)
    return (forward, backward)


def solution(mesh):
    fine = Mesh(mesh.devices.reshape(8, 2, 4, 2, 2), AXES)
    placed = (P(None, COL, ROW), P(ROW, None), P(None, COL, ROW), P(None, COL, None), P(COL, None))
    return jax.shard_map(
        shards,
        mesh=fine,
        in_specs=placed,
        out_specs=(P(None, COL, ROW), P(None, COL, ROW)),
        check_vma=False,
    )
```

time: 471 us -> 86.4 us (0.18)
  waiting for transfers between devices: 356 us -> 27.5 us
  blocking collectives: 72.9 us -> 0 us
  starting transfers between devices: 0.16 us -> 34.4 us
  between operations: 13.8 us -> 0.72 us
  matrix products: 24.6 us -> 11.6 us
  local copies, waits for them, and re-layouts: 0.03 us -> 8.61 us
    reduce_scatter x4 -> x0, waiting for transfers between devices: 356 us -> none  [the longest x1 267 us: shards(): lax.psum_scatter(lax.dot_general(solved_rows, flat, (((0,), (1,)), ((), (...]
    all_gather x3 -> x0, blocking collectives: 72.9 us -> none  [the longest x1 59.5 us: shards(): gathered = lax.all_gather(residual_part[0], 'col', axis=0, tiled=True)]
    ppermute x0 -> x15, starting transfers between devices: none -> 20.2 us  [from_partner(): return lax.ppermute(block, COL, [(s, s ^ flip) for s in range(4)])]
    all_to_all x0 -> x2, waiting for transfers between devices: none -> 14.3 us  [the longest x1 9.04 us: shards(): part = lax.all_to_all(part, ('xl', 'y'), 0, 0, tiled=True).sum(0)]
    all_to_all x0 -> x2, starting transfers between devices: none -> 14.3 us  [the longest x1 8.18 us: shards(): part = lax.all_to_all(part.reshape(8, 8, 512), 'z', 0, 0, tiled=True).sum(0)]
    ppermute x0 -> x15, waiting for transfers between devices: none -> 13.3 us  [from_partner(): return lax.ppermute(block, COL, [(s, s ^ flip) for s in range(4)])]
    dot_general x1, matrix products: 16.8 us -> 7.05 us  [shards(): lax.dot_general(solved_rows, flat, (((0,), (1,)), ((), ())), preferred_el...]
    unnamed x8 -> x5, local copies, waits for them, and re-layouts: 0.02 us -> 5.48 us
  transfers between devices with their start and end apart: 4 -> 17, of which waited for: 4 -> 11; matrix products, arithmetic and copies ran while one was open for 0% -> 5% of each run, Pallas kernels for 0% -> 0%
where the time goes in v1:
time: 86.4 us; the launch traced here: 86.1 us
  starting transfers between devices  34.4 us (40%)
  waiting for transfers between devices  27.5 us (32%)
  matrix products  11.6 us (13%)
  local copies, waits for them, and re-layouts  8.61 us (10%)
  other arithmetic  3.18 us (4%)
    ppermute x15, starting transfers between devices, from_partner(): return lax.ppermute(block, COL, [(s, s ^ flip) for s in range(4)])  20.2 us
    ppermute x15, waiting for transfers between devices, from_partner(): return lax.ppermute(block, COL, [(s, s ^ flip) for s in range(4)])  13.3 us
    all_to_all x1, waiting for transfers between devices, shards(): part = lax.all_to_all(part, ('xl', 'y'), 0, 0, tiled=True).sum(0)  9.04 us
    all_to_all x1, starting transfers between devices, shards(): part = lax.all_to_all(part.reshape(8, 8, 512), 'z', 0, 0, tiled=True).sum(0)  8.18 us
    dot_general x1, matrix products, shards(): lax.dot_general(solved_rows, flat, (((0,), (1,)), ((), ())), preferred_el...  7.05 us
    all_to_all x1, starting transfers between devices, shards(): part = lax.all_to_all(part, ('xl', 'y'), 0, 0, tiled=True).sum(0)  6.08 us
    unnamed x5, local copies, waits for them, and re-layouts  5.48 us
    all_to_all x1, waiting for transfers between devices, shards(): part = lax.all_to_all(part.reshape(8, 8, 512), 'z', 0, 0, tiled=True).sum(0)  5.24 us
  transfers between devices with their start and end apart: 17, of which 11 were waited for; matrix products, arithmetic and copies ran while one was open for 5% of the time, Pallas kernels for 0%

profile of v1, /device:TPU:1, one launch (start us, length us, event | category | flops | bytes accessed | tf_op | source)
XLA Modules:
  0.0 86.1 jit_solution(16803664003784167376)
XLA Ops:
  0.6 5.5 %copy.10 = f32[2048,512]{0,1:T(8,128)} copy(f32[2048,512]{1,0:T(8,128)} %param.6) | data formatting | bytes 8388608 | tf_op args[1]
  6.1 7.0 %convolution_bitcast_fusion = f32[8,8,8,512]{3,2,0,1:T(8,128)S(1)} fusion(f32[8,8,8,2048]{3,2,1,0:T(8,128)} %bitcast.50, f32[512,2048,1,1]{1,0,3,2:T(8,128)} %bitcast.51), kind=kOutput, calls=%fused_computation | convolution fusion | flops 3221225472 | bytes 9437184 | tf_op jit(solution)/shard_map/dot_general | solution.py:47
  13.2 1.1 %copy.14 = f32[8,8,8,512]{3,2,1,0:T(8,128)} copy(f32[8,8,8,512]{3,2,0,1:T(8,128)S(1)} %convolution_bitcast_fusion) | data formatting | bytes 2097152 | tf_op jit(solution)/shard_map/transpose | solution.py:50
  14.2 6.1 %all-to-all-start = ((f32[8,64,512]{2,1,0:T(8,128)}), f32[8,64,512]{2,1,0:T(8,128)S(1)}, u32[]{:S(2)}, u32[]{:S(2)}) async-start(f32[8,64,512]{2,1,0:T(8,128)} %bitcast.52), calls=%async_computation | async-start | bytes 2097152 | tf_op jit(solution)/shard_map/all_to_all | solution.py:51
  20.3 2.0 %constant_dynamic-slice_fusion.3 = (f32[256,256]{1,0:T(8,128)}, f32[256,256]{1,0:T(8,128)}, f32[256,256]{1,0:T(8,128)}) fusion(f32[256,1024]{1,0:T(8,128)} %param.9, s32[]{:T(128)S(6)} %select_n.150, s32[]{:T(128)S(6)} %select_n.148, s32[]{:T(128)S(6)} %select_n.147), kind=kLoop, calls=%fused_computation.60 | loop fusion | bytes 1572876 | tf_op jit(solution)/shard_map/dynamic_slice | solution.py:37
  22.4 3.3 %collective-permute-start.3 = (f32[256,256]{1,0:T(8,128)}, f32[256,256]{1,0:T(8,128)S(1)}, u32[]{:S(2)}, u32[]{:S(2)}) collective-permute-start(f32[256,256]{1,0:T(8,128)} %get-tuple-element.10), channel_id=1, source_target_pairs={{0,3},{1,2},{2,1},{3,0},{4,7},{5,6},{6,5},{7,4},{8,11},{9,10},{10,... | collective-permute-start | bytes 786440 | tf_op jit(solution)/shard_map/ppermute | solution.py:18
  25.7 0.5 collective-permute-start.4
  26.2 0.0 collective-permute-start.5
  26.2 9.0 %all-to-all-done = f32[8,64,512]{2,1,0:T(8,128)S(1)} async-done(((f32[8,64,512]{2,1,0:T(8,128)}), f32[8,64,512]{2,1,0:T(8,128)S(1)}, u32[]{:S(2)}, u32[]{:S(2)}) %all-to-all-start) | async-done | bytes 1048608 | tf_op jit(solution)/shard_map/all_to_all | solution.py:51
  35.2 0.7 reduce_sum.18
  35.9 8.2 %all-to-all-start.1 = ((f32[8,8,512]{2,1,0:T(8,128)}), f32[8,8,512]{2,1,0:T(8,128)S(1)}, u32[]{:S(2)}, u32[]{:S(2)}) async-start(f32[8,8,512]{2,1,0:T(8,128)} %bitcast.9), calls=%async_computation.1 | async-start | bytes 262144 | tf_op jit(solution)/shard_map/all_to_all | solution.py:52
  44.1 0.0 collective-permute-done.3
  44.1 1.6 %collective-permute-done.4 = f32[256,256]{1,0:T(8,128)} collective-permute-done((f32[256,256]{1,0:T(8,128)}, f32[256,256]{1,0:T(8,128)}, u32[]{:S(2)}, u32[]{:S(2)}) %collective-permute-start.4) | collective-permute-done | bytes 262176 | tf_op jit(solution)/shard_map/ppermute | solution.py:18
  45.7 0.0 collective-permute-done.5
  45.7 1.2 %broadcast_select_fusion.5 = (f32[256,256]{1,0:T(8,128)S(1)}, f32[256,256]{1,0:T(8,128)S(1)}, f32[256,256]{1,0:T(8,128)S(1)}, f32[256,256]{1,0:T(8,128)S(1)}) fusion(pred[]{:T(512)S(6)} %eq.15, f32[256,256]{1,0:T(8,128)S(1)} %collective-permute-done.3, f32[256,256]{1,0:T(8,128)} %collective-permute-done.4, pred[]{:T(512)S(6)} %eq.16, ...), kind=kLoop, calls=%fused_computation.25 | loop fusion | flops 524288 | bytes 2097158 | tf_op jit(solution)/shard_map/jit(_where)/select_n | solution.py:24
  46.9 5.2 %all-to-all-done.1 = f32[8,8,512]{2,1,0:T(8,128)S(1)} async-done(((f32[8,8,512]{2,1,0:T(8,128)}), f32[8,8,512]{2,1,0:T(8,128)S(1)}, u32[]{:S(2)}, u32[]{:S(2)}) %all-to-all-start.1) | async-done | bytes 131104 | tf_op jit(solution)/shard_map/all_to_all | solution.py:52
  52.2 4.9 %collective-permute-start = (f32[8,256]{1,0:T(8,128)S(1)}, f32[8,256]{1,0:T(8,128)S(1)}, u32[]{:S(2)}, u32[]{:S(2)}) collective-permute-start(f32[8,256]{1,0:T(8,128)S(1)} %get-tuple-element.14), channel_id=1, source_target_pairs={{0,3},{1,2},{2,1},{3,0},{4,7},{5,6},{6,5},{7,4},{8,11},{9,10},{10,... | collective-permute-start | bytes 24584 | tf_op jit(solution)/shard_map/ppermute | solution.py:18
  57.1 0.5 collective-permute-start.1
  57.6 0.0 collective-permute-start.2
  57.6 0.8 collective-permute-done
  58.4 2.7 %collective-permute-done.1 = f32[8,256]{1,0:T(8,128)S(1)} collective-permute-done((f32[8,256]{1,0:T(8,128)S(1)}, f32[8,256]{1,0:T(8,128)S(1)}, u32[]{:S(2)}, u32[]{:S(2)}) %collective-permute-start.1) | collective-permute-done | bytes 8224 | tf_op jit(solution)/shard_map/ppermute | solution.py:18
  61.1 0.0 collective-permute-done.2
  61.1 0.9 %fusion.7 = f32[8,256]{1,0:T(8,128)S(1)} fusion(f32[2,256,1024]{2,1,0:T(8,128)S(1)} %copy-done, f32[8,256]{1,0:T(8,128)S(1)} %get-tuple-element.18, f32[8,256]{1,0:T(8,128)S(1)} %get-tuple-element.17, f32[8,256]{1,0:T(8,128)S(1)} %get-tuple-element.16, f32[8,256]{1,0:T(8,128)S(1)} %get-tuple-element.15), kind=kOutput, calls=%fused_computation.11 | convolution fusion | flops 25190400 | bytes 1089536 | tf_op jit(solution)/shard_map/dot_general | solution.py:12
  62.0 1.0 %fusion = f32[8,1024]{1,0:T(8,128)S(1)} fusion(f32[8,256]{1,0:T(8,128)S(1)} %fusion.7, f32[256,256]{1,0:T(8,128)S(1)} %get-tuple-element.7, f32[256,256]{1,0:T(8,128)S(1)} %get-tuple-element.6, f32[256,256]{1,0:T(8,128)S(1)} %get-tuple-element.5, f32[256,256]{1,0:T(8,128)S(1)} %get-tuple-element.4, f32[8,256]{1,0:T(8,128)S(1)} %get-tuple-element.21, ...), kind=kOutput, calls=%fused_computation.2 | convolution fusion | flops 25993216 | bytes 1122304 | tf_op jit(solution)/shard_map/dot_general | solution.py:12
  63.0 0.0 collective-permute-start.6
  63.0 1.4 %collective-permute-start.7 = (f32[8,1024]{1,0:T(8,128)S(1)}, f32[8,1024]{1,0:T(8,128)S(1)}, u32[]{:S(2)}, u32[]{:S(2)}) collective-permute-start(f32[8,1024]{1,0:T(8,128)S(1)} %fusion), channel_id=1, source_target_pairs={{0,2},{1,3},{2,0},{3,1},{4,6},{5,7},{6,4},{7,5},{8,10},{9,11},{10,... | collective-permute-start | bytes 98312 | tf_op jit(solution)/shard_map/ppermute | solution.py:18
  64.4 2.3 %collective-permute-start.8 = (f32[8,1024]{1,0:T(8,128)S(1)}, f32[8,1024]{1,0:T(8,128)S(1)}, u32[]{:S(2)}, u32[]{:S(2)}) collective-permute-start(f32[8,1024]{1,0:T(8,128)S(1)} %fusion), channel_id=1, source_target_pairs={{0,3},{1,2},{2,1},{3,0},{4,7},{5,6},{6,5},{7,4},{8,11},{9,10},{10,... | collective-permute-start | bytes 98312 | tf_op jit(solution)/shard_map/ppermute | solution.py:18
  66.7 0.0 collective-permute-done.6
  66.7 0.7 collective-permute-done.7
  67.4 1.9 %collective-permute-done.8 = f32[8,1024]{1,0:T(8,128)S(1)} collective-permute-done((f32[8,1024]{1,0:T(8,128)S(1)}, f32[8,1024]{1,0:T(8,128)S(1)}, u32[]{:S(2)}, u32[]{:S(2)}) %collective-permute-start.8) | collective-permute-done | bytes 32800 | tf_op jit(solution)/shard_map/ppermute | solution.py:18
  69.3 0.9 %fusion.3 = f32[8,256]{1,0:T(8,128)S(1)} fusion(f32[2,256,1024]{2,1,0:T(8,128)S(1)} %copy-done, f32[8,1024]{1,0:T(8,128)S(1)} %collective-permute-done.7, f32[8,1024]{1,0:T(8,128)S(1)} %collective-permute-done.8, f32[8,1024]{1,0:T(8,128)S(1)} %fusion, f32[8,1024]{1,0:T(8,128)S(1)} %collective-permute-done.6), kind=kOutput, calls=%fused_computation.7 | convolution fusion | flops 25190400 | bytes 1187840 | tf_op jit(solution)/shard_map/dot_general | solution.py:12
  70.2 0.6 fusion.1
  70.8 2.3 %collective-permute-start.10 = (f32[8,1024]{1,0:T(8,128)S(1)}, f32[8,1024]{1,0:T(8,128)S(1)}, u32[]{:S(2)}, u32[]{:S(2)}) collective-permute-start(f32[8,1024]{1,0:T(8,128)S(1)} %fusion.1), channel_id=1, source_target_pairs={{0,2},{1,3},{2,0},{3,1},{4,6},{5,7},{6,4},{7,5},{8,10},{9,11},{10,... | collective-permute-start | bytes 98312 | tf_op jit(solution)/shard_map/ppermute | solution.py:18
  73.1 1.2 %collective-permute-start.11 = (f32[8,1024]{1,0:T(8,128)S(1)}, f32[8,1024]{1,0:T(8,128)S(1)}, u32[]{:S(2)}, u32[]{:S(2)}) collective-permute-start(f32[8,1024]{1,0:T(8,128)S(1)} %fusion.1), channel_id=1, source_target_pairs={{0,3},{1,2},{2,1},{3,0},{4,7},{5,6},{6,5},{7,4},{8,11},{9,10},{10,... | collective-permute-start | bytes 98312 | tf_op jit(solution)/shard_map/ppermute | solution.py:18
  74.3 0.0 collective-permute-start.9
  74.3 0.6 maximum_bitcast_fusion
  74.9 0.2 collective-permute-done.10
  75.1 3.5 %collective-permute-done.11 = f32[8,1024]{1,0:T(8,128)S(1)} collective-permute-done((f32[8,1024]{1,0:T(8,128)S(1)}, f32[8,1024]{1,0:T(8,128)S(1)}, u32[]{:S(2)}, u32[]{:S(2)}) %collective-permute-start.11) | collective-permute-done | bytes 32800 | tf_op jit(solution)/shard_map/ppermute | solution.py:18
  78.6 0.0 collective-permute-done.9
  78.6 0.5 convolution_subtract_fusion
  79.2 0.6 fusion.5
  79.8 0.5 collective-permute-start.12
  80.2 0.6 collective-permute-start.13
  80.9 2.7 %collective-permute-start.14 = (f32[8,256]{1,0:T(8,128)S(1)}, f32[8,256]{1,0:T(8,128)S(1)}, u32[]{:S(2)}, u32[]{:S(2)}) collective-permute-start(f32[8,256]{1,0:T(8,128)S(1)} %get-tuple-element.12), channel_id=1, source_target_pairs={{0,3},{1,2},{2,1},{3,0},{4,7},{5,6},{6,5},{7,4},{8,11},{9,10},{10,... | collective-permute-start | bytes 24584 | tf_op jit(solution)/shard_map/ppermute | solution.py:18
  83.5 0.0 collective-permute-done.12
  83.5 0.7 collective-permute-done.13
  84.2 1.2 %collective-permute-done.14 = f32[8,256]{1,0:T(8,128)S(1)} collective-permute-done((f32[8,256]{1,0:T(8,128)S(1)}, f32[8,256]{1,0:T(8,128)S(1)}, u32[]{:S(2)}, u32[]{:S(2)}) %collective-permute-start.14) | collective-permute-done | bytes 8224 | tf_op jit(solution)/shard_map/ppermute | solution.py:18
  85.5 0.6 maximum_bitcast_fusion.1
  (12 shorter events, 0.1 us)
Async XLA Ops:
  14.2 37.9 %copy-start.1 = (f32[2,256,8]{1,2,0:T(8,128)S(1)}, f32[2,256,8]{1,2,0:T(8,128)}, u32[]{:S(2)}) copy-start(f32[2,256,8]{1,2,0:T(8,128)} %param.7) | copy-start | bytes 49156
  14.2 46.8 %copy-start = (f32[2,256,1024]{2,1,0:T(8,128)S(1)}, f32[2,256,1024]{2,1,0:T(8,128)}, u32[]{:S(2)}) copy-start(f32[2,256,1024]{2,1,0:T(8,128)} %param.8) | copy-start | bytes 6291460
  14.2 21.0 %all-to-all-start = ((f32[8,64,512]{2,1,0:T(8,128)}), f32[8,64,512]{2,1,0:T(8,128)S(1)}, u32[]{:S(2)}, u32[]{:S(2)}) async-start(f32[8,64,512]{2,1,0:T(8,128)} %bitcast.52), calls=%async_computation | async-start | bytes 2097152 | tf_op jit(solution)/shard_map/all_to_all | solution.py:51
  22.4 21.8 %collective-permute-start.3 = (f32[256,256]{1,0:T(8,128)}, f32[256,256]{1,0:T(8,128)S(1)}, u32[]{:S(2)}, u32[]{:S(2)}) collective-permute-start(f32[256,256]{1,0:T(8,128)} %get-tuple-element.10), channel_id=1, source_target_pairs={{0,3},{1,2},{2,1},{3,0},{4,7},{5,6},{6,5},{7,4},{8,11},{9,10},{10,... | collective-permute-start | bytes 786440 | tf_op jit(solution)/shard_map/ppermute | solution.py:18
  25.7 20.0 %collective-permute-start.4 = (f32[256,256]{1,0:T(8,128)}, f32[256,256]{1,0:T(8,128)}, u32[]{:S(2)}, u32[]{:S(2)}) collective-permute-start(f32[256,256]{1,0:T(8,128)} %get-tuple-element.9), channel_id=1, source_target_pairs={{0,2},{1,3},{2,0},{3,1},{4,6},{5,7},{6,4},{7,5},{8,10},{9,11},{10,... | collective-permute-start | bytes 786440 | tf_op jit(solution)/shard_map/ppermute | solution.py:18
  26.2 19.5 %collective-permute-start.5 = (f32[256,256]{1,0:T(8,128)}, f32[256,256]{1,0:T(8,128)}, u32[]{:S(2)}, u32[]{:S(2)}) collective-permute-start(f32[256,256]{1,0:T(8,128)} %get-tuple-element.8), channel_id=1, source_target_pairs={{0,1},{1,0},{2,3},{3,2},{4,5},{5,4},{6,7},{7,6},{8,9},{9,8},{10,11... | collective-permute-start | bytes 786440 | tf_op jit(solution)/shard_map/ppermute | solution.py:18
  35.9 16.2 %all-to-all-start.1 = ((f32[8,8,512]{2,1,0:T(8,128)}), f32[8,8,512]{2,1,0:T(8,128)S(1)}, u32[]{:S(2)}, u32[]{:S(2)}) async-start(f32[8,8,512]{2,1,0:T(8,128)} %bitcast.9), calls=%async_computation.1 | async-start | bytes 262144 | tf_op jit(solution)/shard_map/all_to_all | solution.py:52
  52.2 6.2 %collective-permute-start = (f32[8,256]{1,0:T(8,128)S(1)}, f32[8,256]{1,0:T(8,128)S(1)}, u32[]{:S(2)}, u32[]{:S(2)}) collective-permute-start(f32[8,256]{1,0:T(8,128)S(1)} %get-tuple-element.14), channel_id=1, source_target_pairs={{0,3},{1,2},{2,1},{3,0},{4,7},{5,6},{6,5},{7,4},{8,11},{9,10},{10,... | collective-permute-start | bytes 24584 | tf_op jit(solution)/shard_map/ppermute | solution.py:18
  57.1 4.0 %collective-permute-start.1 = (f32[8,256]{1,0:T(8,128)S(1)}, f32[8,256]{1,0:T(8,128)S(1)}, u32[]{:S(2)}, u32[]{:S(2)}) collective-permute-start(f32[8,256]{1,0:T(8,128)S(1)} %get-tuple-element.14), channel_id=1, source_target_pairs={{0,2},{1,3},{2,0},{3,1},{4,6},{5,7},{6,4},{7,5},{8,10},{9,11},{10,... | collective-permute-start | bytes 24584 | tf_op jit(solution)/shard_map/ppermute | solution.py:18
  57.6 3.5 %collective-permute-start.2 = (f32[8,256]{1,0:T(8,128)S(1)}, f32[8,256]{1,0:T(8,128)S(1)}, u32[]{:S(2)}, u32[]{:S(2)}) collective-permute-start(f32[8,256]{1,0:T(8,128)S(1)} %get-tuple-element.14), channel_id=1, source_target_pairs={{0,1},{1,0},{2,3},{3,2},{4,5},{5,4},{6,7},{7,6},{8,9},{9,8},{10,11... | collective-permute-start | bytes 24584 | tf_op jit(solution)/shard_map/ppermute | solution.py:18
  63.0 3.7 %collective-permute-start.6 = (f32[8,1024]{1,0:T(8,128)S(1)}, f32[8,1024]{1,0:T(8,128)S(1)}, u32[]{:S(2)}, u32[]{:S(2)}) collective-permute-start(f32[8,1024]{1,0:T(8,128)S(1)} %fusion), channel_id=1, source_target_pairs={{0,1},{1,0},{2,3},{3,2},{4,5},{5,4},{6,7},{7,6},{8,9},{9,8},{10,11... | collective-permute-start | bytes 98312 | tf_op jit(solution)/shard_map/ppermute | solution.py:18
  63.0 4.4 %collective-permute-start.7 = (f32[8,1024]{1,0:T(8,128)S(1)}, f32[8,1024]{1,0:T(8,128)S(1)}, u32[]{:S(2)}, u32[]{:S(2)}) collective-permute-start(f32[8,1024]{1,0:T(8,128)S(1)} %fusion), channel_id=1, source_target_pairs={{0,2},{1,3},{2,0},{3,1},{4,6},{5,7},{6,4},{7,5},{8,10},{9,11},{10,... | collective-permute-start | bytes 98312 | tf_op jit(solution)/shard_map/ppermute | solution.py:18
  64.4 4.9 %collective-permute-start.8 = (f32[8,1024]{1,0:T(8,128)S(1)}, f32[8,1024]{1,0:T(8,128)S(1)}, u32[]{:S(2)}, u32[]{:S(2)}) collective-permute-start(f32[8,1024]{1,0:T(8,128)S(1)} %fusion), channel_id=1, source_target_pairs={{0,3},{1,2},{2,1},{3,0},{4,7},{5,6},{6,5},{7,4},{8,11},{9,10},{10,... | collective-permute-start | bytes 98312 | tf_op jit(solution)/shard_map/ppermute | solution.py:18
  70.8 4.3 %collective-permute-start.10 = (f32[8,1024]{1,0:T(8,128)S(1)}, f32[8,1024]{1,0:T(8,128)S(1)}, u32[]{:S(2)}, u32[]{:S(2)}) collective-permute-start(f32[8,1024]{1,0:T(8,128)S(1)} %fusion.1), channel_id=1, source_target_pairs={{0,2},{1,3},{2,0},{3,1},{4,6},{5,7},{6,4},{7,5},{8,10},{9,11},{10,... | collective-permute-start | bytes 98312 | tf_op jit(solution)/shard_map/ppermute | solution.py:18
  73.1 5.5 %collective-permute-start.11 = (f32[8,1024]{1,0:T(8,128)S(1)}, f32[8,1024]{1,0:T(8,128)S(1)}, u32[]{:S(2)}, u32[]{:S(2)}) collective-permute-start(f32[8,1024]{1,0:T(8,128)S(1)} %fusion.1), channel_id=1, source_target_pairs={{0,3},{1,2},{2,1},{3,0},{4,7},{5,6},{6,5},{7,4},{8,11},{9,10},{10,... | collective-permute-start | bytes 98312 | tf_op jit(solution)/shard_map/ppermute | solution.py:18
  74.3 4.3 %collective-permute-start.9 = (f32[8,1024]{1,0:T(8,128)S(1)}, f32[8,1024]{1,0:T(8,128)S(1)}, u32[]{:S(2)}, u32[]{:S(2)}) collective-permute-start(f32[8,1024]{1,0:T(8,128)S(1)} %fusion.1), channel_id=1, source_target_pairs={{0,1},{1,0},{2,3},{3,2},{4,5},{5,4},{6,7},{7,6},{8,9},{9,8},{10,11... | collective-permute-start | bytes 98312 | tf_op jit(solution)/shard_map/ppermute | solution.py:18
  79.8 3.7 %collective-permute-start.12 = (f32[8,256]{1,0:T(8,128)S(1)}, f32[8,256]{1,0:T(8,128)S(1)}, u32[]{:S(2)}, u32[]{:S(2)}) collective-permute-start(f32[8,256]{1,0:T(8,128)S(1)} %get-tuple-element.11), channel_id=1, source_target_pairs={{0,1},{1,0},{2,3},{3,2},{4,5},{5,4},{6,7},{7,6},{8,9},{9,8},{10,11... | collective-permute-start | bytes 24584 | tf_op jit(solution)/shard_map/ppermute | solution.py:18
  80.2 4.0 %collective-permute-start.13 = (f32[8,256]{1,0:T(8,128)S(1)}, f32[8,256]{1,0:T(8,128)S(1)}, u32[]{:S(2)}, u32[]{:S(2)}) collective-permute-start(f32[8,256]{1,0:T(8,128)S(1)} %get-tuple-element.13), channel_id=1, source_target_pairs={{0,2},{1,3},{2,0},{3,1},{4,6},{5,7},{6,4},{7,5},{8,10},{9,11},{10,... | collective-permute-start | bytes 24584 | tf_op jit(solution)/shard_map/ppermute | solution.py:18
  80.9 4.6 %collective-permute-start.14 = (f32[8,256]{1,0:T(8,128)S(1)}, f32[8,256]{1,0:T(8,128)S(1)}, u32[]{:S(2)}, u32[]{:S(2)}) collective-permute-start(f32[8,256]{1,0:T(8,128)S(1)} %get-tuple-element.12), channel_id=1, source_target_pairs={{0,3},{1,2},{2,1},{3,0},{4,7},{5,6},{6,5},{7,4},{8,11},{9,10},{10,... | collective-permute-start | bytes 24584 | tf_op jit(solution)/shard_map/ppermute | solution.py:18

commit v2 on v1

v2 whole, which is shorter than its diff:
```python
import jax
import jax.numpy as jnp
from jax import lax
from jax.experimental import pallas as pl
from jax.experimental.pallas import tpu as pltpu
from jax.sharding import Mesh, PartitionSpec as P

AXES = ("z", "xl", "y", "xh", "core")
ROW = ("z", "xl", "y")
COL = ("xh", "core")
NEAR = ("xl", "xh", "core")
DEPTH = 256
STEPS = 2048 // DEPTH


def split(block):
    high = block.astype(jnp.bfloat16)
    return high, (block - high.astype(jnp.float32)).astype(jnp.bfloat16)


def product_kernel(factor_hbm, solved_hbm, out_ref, factor_ref, solved_ref, sem):
    copies = []
    for k in range(STEPS):
        span = pl.ds(k * DEPTH, DEPTH)
        pair = (
            pltpu.make_async_copy(factor_hbm.at[:, span], factor_ref.at[:, span], sem.at[0, k]),
            pltpu.make_async_copy(solved_hbm.at[span, :], solved_ref.at[span, :], sem.at[1, k]),
        )
        pair[0].start()
        pair[1].start()
        copies.append(pair)
    for k in range(STEPS):
        copies[k][0].wait()
        copies[k][1].wait()
        fh, fl = split(factor_ref[:, k * DEPTH : (k + 1) * DEPTH])
        sh, sl = split(solved_ref[k * DEPTH : (k + 1) * DEPTH, :])
        term = jnp.dot(
            jnp.concatenate([fh, fh, fl], axis=1),
            jnp.concatenate([sh, sl, sh], axis=0),
            preferred_element_type=jnp.float32,
        )
        if k == 0:
            out_ref[...] = term
        else:
            out_ref[...] += term


def product(flat, solved_rows):
    return pl.pallas_call(
        product_kernel,
        in_specs=[pl.BlockSpec(memory_space=pl.ANY)] * 2,
        out_specs=pl.BlockSpec(memory_space=pltpu.VMEM),
        out_shape=pltpu.VMEM((512, 512), jnp.float32),
        scratch_shapes=[
            pltpu.VMEM((512, 2048), jnp.float32),
            pltpu.VMEM((2048, 512), jnp.float32),
            pltpu.SemaphoreType.DMA((2, STEPS)),
        ],
        compiler_params=pltpu.CompilerParams(vmem_limit_bytes=20 << 20),
        cost_estimate=pl.CostEstimate(flops=6 * 512 * 512 * 2048, bytes_accessed=9 << 20, transcendentals=0),
        name="product",
    )(pltpu.with_memory_space_constraint(flat, pltpu.HBM), pltpu.with_memory_space_constraint(solved_rows, pltpu.HBM))


def place_kernel(at_ref, update_ref, right_ref, slab_ref, out_ref, copy_ref):
    copy_ref[...] = slab_ref[...]
    turned = -update_ref[...].T
    for z in range(8):
        for p in range(8):
            out_ref[p, pl.ds(8 * z, 8), :] = turned[64 * z + 8 * p : 64 * z + 8 * p + 8, :]
    rows = pl.ds(pl.multiple_of(at_ref[1] * 8, 8), 8)
    out_ref[at_ref[0], rows, 0:256] += right_ref[0]
    out_ref[at_ref[0], rows, 256:512] += right_ref[1]


def place(at, update, right, slab):
    vmem = pl.BlockSpec(memory_space=pltpu.VMEM)
    return pl.pallas_call(
        place_kernel,
        in_specs=[pl.BlockSpec(memory_space=pltpu.SMEM), vmem, vmem, vmem],
        out_specs=[vmem, vmem],
        out_shape=[jax.ShapeDtypeStruct((8, 64, 512), jnp.float32), jax.ShapeDtypeStruct(slab.shape, jnp.float32)],
        compiler_params=pltpu.CompilerParams(vmem_limit_bytes=8 << 20),
        cost_estimate=pl.CostEstimate(flops=1 << 18, bytes_accessed=2 << 20, transcendentals=0),
        name="place",
    )(at, update, right, slab)


def sum_after(parts, awaited):
    vmem = pl.BlockSpec(memory_space=pltpu.VMEM)

    def kernel(parts_ref, *refs):
        total = parts_ref[0]
        for k in range(1, 8):
            total = total + parts_ref[k]
        refs[-1][...] = total

    return pl.pallas_call(
        kernel,
        in_specs=[vmem] + [pl.BlockSpec(memory_space=pl.ANY)] * len(awaited),
        out_specs=vmem,
        out_shape=jax.ShapeDtypeStruct(parts.shape[1:], jnp.float32),
        cost_estimate=pl.CostEstimate(flops=1 << 15, bytes_accessed=1 << 17, transcendentals=0),
        name="sum_after",
    )(parts, *awaited)


def exact(left, right, dims):
    return lax.dot_general(
        left, right, (dims, ((), ())), preferred_element_type=jnp.float32, precision=lax.Precision.HIGHEST
    )


def near(block):
    return lax.ppermute(block, "core", [(0, 1), (1, 0)])


def far(block):
    return lax.ppermute(block, NEAR, [(s, s ^ 6) for s in range(8)])


def from_col(block, flip):
    return lax.ppermute(block, COL, [(s, s ^ flip) for s in range(4)])


def from_quad(block, turn):
    pairs = []
    for z in range(8):
        for xl in range(2):
            for col in range(4):
                k = (z % 4 + turn) % 4
                step = (col - z) % 4
                step = {0: 0, 1: 1, 2: -2 if col % 2 else 2, 3: -1}[step]
                source = ((z + step) % 8 * 2 + (xl ^ (col >> 1) ^ (k >> 1))) * 4 + k
                pairs.append((source, (z * 2 + xl) * 4 + col))
    return lax.ppermute(block, ("z", "xl", "xh", "core"), pairs)


def in_order(pieces, mine):
    high, low = mine // 2, mine % 2
    a = [jnp.where(low == 1, pieces[k ^ 1], pieces[k]) for k in range(4)]
    return [jnp.where(high == 1, a[k ^ 2], a[k]) for k in range(4)]


def turned(pieces, quad):
    a = [jnp.where(quad % 2 == 1, pieces[k - 1], pieces[k]) for k in range(4)]
    return [jnp.where(quad // 2 == 1, a[k - 2], a[k]) for k in range(4)]


def block_of(array, index):
    return lax.dynamic_slice_in_dim(array, index * 256, 256, 1)


def added(blocks):
    return (blocks[0] + blocks[1]) + (blocks[2] + blocks[3])


def shards(factor_rows, solved_rows, right_side, inverse, coupling):
    mine = lax.axis_index(COL)
    quad = lax.axis_index("z") % 4
    at = jnp.stack([lax.axis_index(("xl", "y")), lax.axis_index("z")])

    slab = lax.dynamic_slice(inverse, (0, 0, quad * 256), (1, 256, 256))[0]
    slab_far = far(slab)
    update = product(factor_rows.reshape(512, 2048), solved_rows)
    part, slab_far = place(at, update, right_side.transpose(0, 2, 1), slab_far)
    part = lax.all_to_all(part, ("xl", "y"), 0, 0, tiled=True)
    whole = jnp.concatenate(in_order([slab, near(slab), slab_far, near(slab_far)], mine), axis=0)
    middle = exact(coupling, whole, ((1,), (0,)))
    part = sum_after(part, [middle])
    columns = [from_quad(middle, k) for k in range(4)]
    part = lax.all_to_all(part.reshape(8, 8, 512), "z", 0, 0, tiled=True)
    r = sum_after(part, columns)
    columns = jnp.concatenate(turned(columns, quad), axis=0)

    r0, r1 = r[:, :256], r[:, 256:]
    s = jnp.concatenate([jnp.where(mine == k, r1, 0.0) for k in range(4)], axis=1) - exact(r0, columns, ((1,), (1,)))
    sent = jnp.concatenate([r0, s], axis=1)
    got = [sent] + [from_col(sent, k) for k in (1, 2, 3)]
    f0 = exact(jnp.concatenate(in_order([g[:, :256] for g in got], mine), axis=1), inverse[0], ((1,), (1,)))
    f1 = exact(added([g[:, 256:] for g in got]), inverse[1], ((1,), (1,)))
    b0 = exact(f0, inverse[0], ((1,), (0,)))
    b1 = exact(f1, inverse[1], ((1,), (0,)))
    sent = [jnp.concatenate([block_of(b0, mine ^ k), b1], axis=1) for k in range(4)]
    got = [sent[0]] + [from_col(sent[k], k) for k in (1, 2, 3)]
    b = added(got)
    b1 = b[:, 256:]
    b0 = b[:, :256] - exact(b1, columns, ((1,), (0,)))
    forward = jnp.stack([f0, f1])
    backward = jnp.stack([b0, block_of(b1, mine)])
    return (forward.transpose(0, 2, 1), backward.transpose(0, 2, 1))


def solution(mesh):
    fine = Mesh(mesh.devices.reshape(8, 2, 4, 2, 2), AXES)
    placed = (P(None, COL, ROW), P(ROW, None), P(None, COL, ROW), P(None, COL, None), P(COL, None))
    return jax.shard_map(
        shards,
        mesh=fine,
        in_specs=placed,
        out_specs=(P(None, COL, ROW), P(None, COL, ROW)),
        check_vma=False,
    )
```

time: 86.4 us -> 79.1 us (0.916)
  waiting for transfers between devices: 27.5 us -> 11.3 us
  Pallas kernels: 0 us -> 10.5 us
  starting transfers between devices: 34.4 us -> 40.7 us
  matrix products: 11.6 us -> 6.81 us
  local copies, waits for them, and re-layouts: 8.61 us -> 4.28 us
  other arithmetic: 3.18 us -> 4.21 us
    pallas_call x0 -> x4, Pallas kernels: none -> 10.5 us  [the longest x1 5.17 us: product(): pl.pallas_call(product_kernel, in_specs=[pl.BlockSpec(memory_space=pl.ANY...]
    all_to_all x2, waiting for transfers between devices: 14.3 us -> 5.09 us  [the longest x1 5.08 us: shards(): part = lax.all_to_all(part.reshape(8, 8, 512), 'z', 0, 0, tiled=True)]
    ppermute x15 -> x13, starting transfers between devices: 20.2 us -> 29 us  [the longest x4 13.5 us: from_quad(): return lax.ppermute(block, ('z', 'xl', 'xh', 'core'), pairs)]
    ppermute x15 -> x13, waiting for transfers between devices: 13.3 us -> 6.25 us  [the longest x6 6.24 us: from_col(): return lax.ppermute(block, COL, [(s, s ^ flip) for s in range(4)])]
    dot_general x7, matrix products: 11.6 us -> 6.81 us  [exact(): lax.dot_general(left, right, (dims, ((), ())), preferred_element_type=jnp...]
    all_to_all x2, starting transfers between devices: 14.3 us -> 11.7 us  [the longest x1 7.53 us: shards(): part = lax.all_to_all(part.reshape(8, 8, 512), 'z', 0, 0, tiled=True)]
    unnamed x5 -> x30, local copies, waits for them, and re-layouts: 5.48 us -> 3.21 us
    dynamic_slice x2 -> x1, local copies, waits for them, and re-layouts: 2.05 us -> 0.01 us  [block_of(): return lax.dynamic_slice_in_dim(array, index * 256, 256, 1)]
  transfers between devices with their start and end apart: 17 -> 15, of which waited for: 11 -> 5; matrix products, arithmetic and copies ran while one was open for 5% -> 5% of each run, Pallas kernels for 0% -> 11%
where the time goes in v2:
time: 79.1 us; the launch traced here: 78.7 us
  starting transfers between devices  40.7 us (51%)
  waiting for transfers between devices  11.3 us (14%)
  Pallas kernels  10.5 us (13%)
  matrix products  6.81 us (9%)
  local copies, waits for them, and re-layouts  4.28 us (5%)
  other arithmetic  4.21 us (5%)
  between operations  0.91 us (1%)
    ppermute x4, starting transfers between devices, from_quad(): return lax.ppermute(block, ('z', 'xl', 'xh', 'core'), pairs)  13.5 us
    ppermute x6, starting transfers between devices, from_col(): return lax.ppermute(block, COL, [(s, s ^ flip) for s in range(4)])  9.91 us
    all_to_all x1, starting transfers between devices, shards(): part = lax.all_to_all(part.reshape(8, 8, 512), 'z', 0, 0, tiled=True)  7.53 us
    dot_general x7, matrix products, exact(): lax.dot_general(left, right, (dims, ((), ())), preferred_element_type=jnp...  6.81 us
    ppermute x6, waiting for transfers between devices, from_col(): return lax.ppermute(block, COL, [(s, s ^ flip) for s in range(4)])  6.24 us
    pallas_call x1, Pallas kernels, product(): pl.pallas_call(product_kernel, in_specs=[pl.BlockSpec(memory_space=pl.ANY...  5.17 us
    all_to_all x1, waiting for transfers between devices, shards(): part = lax.all_to_all(part.reshape(8, 8, 512), 'z', 0, 0, tiled=True)  5.08 us
    all_to_all x1, starting transfers between devices, shards(): part = lax.all_to_all(part, ('xl', 'y'), 0, 0, tiled=True)  4.13 us
  transfers between devices with their start and end apart: 15, of which 5 were waited for; matrix products, arithmetic and copies ran while one was open for 5% of the time, Pallas kernels for 11%

profile of v2, /device:TPU:1, one launch (start us, length us, event | category | flops | bytes accessed | tf_op | source)
XLA Modules:
  0.0 78.7 jit_solution(7780943181645178895)
XLA Ops:
  0.6 0.0 copy-start
  0.7 1.1 %dynamic-slice_bitcast_fusion = f32[256,256]{1,0:T(8,128)S(1)} fusion(f32[2,256,1024]{2,1,0:T(8,128)} %param.8, s32[]{:T(128)S(6)} %select_n.193), kind=kLoop, calls=%fused_computation.23 | loop fusion | bytes 524292 | tf_op jit(solution)/shard_map/squeeze | solution.py:163
  1.7 3.4 %collective-permute-start = (f32[256,256]{1,0:T(8,128)S(1)}, f32[256,256]{1,0:T(8,128)S(1)}, u32[]{:S(2)}, u32[]{:S(2)}) collective-permute-start(f32[256,256]{1,0:T(8,128)S(1)} %dynamic-slice_bitcast_fusion), channel_id=1, source_target_pairs={{0,18},{1,19},{2,16},{3,17},{16,2},{17,3},{18,0},{19,1},{4,22},{5,... | collective-permute-start | bytes 786440 | tf_op jit(solution)/shard_map/ppermute | solution.py:119
  5.1 1.0 %collective-permute-start.2 = (f32[256,256]{1,0:T(8,128)S(1)}, f32[256,256]{1,0:T(8,128)S(1)}, u32[]{:S(2)}, u32[]{:S(2)}) collective-permute-start(f32[256,256]{1,0:T(8,128)S(1)} %dynamic-slice_bitcast_fusion), channel_id=1, source_target_pairs={{0,1},{1,0},{2,3},{3,2},{4,5},{5,4},{6,7},{7,6},{8,9},{9,8},{10,11... | collective-permute-start | bytes 786440 | tf_op jit(solution)/shard_map/ppermute | solution.py:115
  6.1 0.1 pad_add_fusion.at_ref
  6.2 5.2 %product.1.update_ref = f32[512,512]{1,0:T(8,128)S(1)} custom-call(f32[512,2048]{1,0:T(8,128)} %bitcast.38, f32[2048,512]{1,0:T(8,128)} %solved_hbm.1), custom_call_target="tpu_custom_call" | custom-call | flops 3221225472 | bytes 9437184 | tf_op jit(solution)/shard_map/product/pallas_call | solution.py:49
  11.4 1.9 %place.1 = (f32[8,64,512]{2,1,0:T(8,128)}, f32[256,256]{1,0:T(8,128)S(1)}) custom-call(s32[2]{0:T(128)S(1)} %pad_add_fusion.at_ref, f32[512,512]{1,0:T(8,128)S(1)} %product.1.update_ref, f32[2,8,256]{2,1,0:T(8,128)S(1)} %bitcast.34, f32[256,256]{1,0:T(8,128)S(1)} %collective-permute-done.slab_ref), custom_call_target="tpu_custom_call" | custom-call | flops 262144 | bytes 2097152 | tf_op jit(solution)/shard_map/place/pallas_call | solution.py:78
  13.2 1.3 %collective-permute-start.1 = (f32[256,256]{1,0:T(8,128)S(1)}, f32[256,256]{1,0:T(8,128)S(1)}, u32[]{:S(2)}, u32[]{:S(2)}) collective-permute-start(f32[256,256]{1,0:T(8,128)S(1)} %get-tuple-element.5), channel_id=1, source_target_pairs={{0,1},{1,0},{2,3},{3,2},{4,5},{5,4},{6,7},{7,6},{8,9},{9,8},{10,11... | collective-permute-start | bytes 786440 | tf_op jit(solution)/shard_map/ppermute | solution.py:115
  14.5 4.1 %all-to-all-start = ((f32[8,64,512]{2,1,0:T(8,128)}), f32[8,64,512]{2,1,0:T(8,128)S(1)}, u32[]{:S(2)}, u32[]{:S(2)}) async-start(f32[8,64,512]{2,1,0:T(8,128)} %get-tuple-element.4), calls=%async_computation | async-start | bytes 2097152 | tf_op jit(solution)/shard_map/all_to_all | solution.py:167
  18.6 0.0 collective-permute-done.1
  18.6 1.1 %broadcast_select_fusion.15 = (f32[256,256]{1,0:T(8,128)S(1)}, f32[256,256]{1,0:T(8,128)S(1)}, f32[256,256]{1,0:T(8,128)S(1)}, f32[256,256]{1,0:T(8,128)S(1)}) fusion(pred[]{:T(512)S(6)} %eq.24, f32[256,256]{1,0:T(8,128)S(1)} %collective-permute-done.1, f32[256,256]{1,0:T(8,128)S(1)} %get-tuple-element.5, pred[]{:T(512)S(6)} %eq.25, ...), kind=kLoop, calls=%fused_computation.39 | loop fusion | flops 524288 | bytes 2097158 | tf_op jit(solution)/shard_map/jit(_where)/select_n | solution.py:142
  19.7 1.1 %convolution_bitcast_fusion.refs_0_ = f32[256,256]{1,0:T(8,128)S(1)} fusion(f32[256,1024]{1,0:T(8,128)S(1)} %copy-done, f32[256,256]{1,0:T(8,128)S(1)} %get-tuple-element.13, f32[256,256]{1,0:T(8,128)S(1)} %get-tuple-element.12, f32[256,256]{1,0:T(8,128)S(1)} %get-tuple-element.11, f32[256,256]{1,0:T(8,128)S(1)} %get-tuple-element.10), kind=kOutput, calls=%fused_computation | convolution fusion | flops 806092800 | bytes 2359296 | tf_op jit(solution)/shard_map/dot_general | solution.py:109
  20.8 3.7 %collective-permute-start.3 = (f32[256,256]{1,0:T(8,128)S(1)}, f32[256,256]{1,0:T(8,128)S(1)}, u32[]{:S(2)}, u32[]{:S(2)}) collective-permute-start(f32[256,256]{1,0:T(8,128)S(1)} %convolution_bitcast_fusion.refs_0_), channel_id=1, source_target_pairs={{0,0},{32,1},{80,2},{240,3},{16,16},{48,17},{64,18},{224,19},{1,32... | collective-permute-start | bytes 786440 | tf_op jit(solution)/shard_map/ppermute | solution.py:136
  24.5 0.1 collective-permute-start.4
  24.6 6.5 %collective-permute-start.5 = (f32[256,256]{1,0:T(8,128)S(1)}, f32[256,256]{1,0:T(8,128)S(1)}, u32[]{:S(2)}, u32[]{:S(2)}) collective-permute-start(f32[256,256]{1,0:T(8,128)S(1)} %convolution_bitcast_fusion.refs_0_), channel_id=1, source_target_pairs={{18,0},{50,1},{66,2},{226,3},{2,16},{34,17},{82,18},{242,19},{19,3... | collective-permute-start | bytes 786440 | tf_op jit(solution)/shard_map/ppermute | solution.py:136
  31.1 3.2 %collective-permute-start.6 = (f32[256,256]{1,0:T(8,128)S(1)}, f32[256,256]{1,0:T(8,128)S(1)}, u32[]{:S(2)}, u32[]{:S(2)}) collective-permute-start(f32[256,256]{1,0:T(8,128)S(1)} %convolution_bitcast_fusion.refs_0_), channel_id=1, source_target_pairs={{19,0},{51,1},{67,2},{227,3},{3,16},{35,17},{83,18},{243,19},{0,32... | collective-permute-start | bytes 786440 | tf_op jit(solution)/shard_map/ppermute | solution.py:136
  34.3 1.0 %copy-done.3 = f32[8,64,512]{2,1,0:T(8,128)} copy-done((f32[8,64,512]{2,1,0:T(8,128)}, f32[8,64,512]{2,1,0:T(8,128)S(1)}, u32[]{:S(2)}) %copy-start.3) | copy-done | bytes 1048600
  35.2 1.9 %sum_after.2 = f32[64,512]{1,0:T(8,128)} custom-call(f32[8,64,512]{2,1,0:T(8,128)} %copy-done.3, f32[256,256]{1,0:T(8,128)} %copy-done.4), custom_call_target="tpu_custom_call" | custom-call | flops 32768 | bytes 131072 | tf_op jit(solution)/shard_map/sum_after/pallas_call | solution.py:98
  37.2 7.5 %all-to-all-start.1 = ((f32[8,8,512]{2,1,0:T(8,128)}), f32[8,8,512]{2,1,0:T(8,128)S(1)}, u32[]{:S(2)}, u32[]{:S(2)}) async-start(f32[8,8,512]{2,1,0:T(8,128)} %bitcast.35), calls=%async_computation.1 | async-start | bytes 262144 | tf_op jit(solution)/shard_map/all_to_all | solution.py:172
  44.7 0.0 collective-permute-done.4.refs_1_
  44.8 0.0 collective-permute-done.5.refs_2_
  44.8 0.7 copy-done.6
  45.5 0.1 copy-done.7
  45.6 0.7 copy-done.8
  46.3 1.1 %broadcast_select_fusion.7 = (f32[256,256]{1,0:T(8,128)}, f32[256,256]{1,0:T(8,128)}, f32[256,256]{1,0:T(8,128)}, f32[256,256]{1,0:T(8,128)}) fusion(pred[]{:T(512)S(6)} %eq.58, f32[256,256]{1,0:T(8,128)S(1)} %collective-permute-done.4.refs_1_, f32[256,256]{1,0:T(8,128)S(1)} %collective-permute-done.5.refs_2_, pred[]{:T(512)S(6)} %eq.59, ...), kind=kLoop, calls=%fused_computation.31 | loop fusion | flops 524288 | bytes 2097154 | tf_op jit(solution)/shard_map/jit(_where)/select_n | solution.py:147
  47.4 5.1 %all-to-all-done.1.parts_ref = f32[8,8,512]{2,1,0:T(8,128)S(1)} async-done(((f32[8,8,512]{2,1,0:T(8,128)}), f32[8,8,512]{2,1,0:T(8,128)S(1)}, u32[]{:S(2)}, u32[]{:S(2)}) %all-to-all-start.1) | async-done | bytes 131104 | tf_op jit(solution)/shard_map/all_to_all | solution.py:172
  52.5 0.7 copy-done.9
  53.2 1.5 %sum_after.3 = f32[8,512]{1,0:T(8,128)} custom-call(f32[8,8,512]{2,1,0:T(8,128)} %copy-done.9, f32[256,256]{1,0:T(8,128)} %copy-done.5, f32[256,256]{1,0:T(8,128)} %copy-done.6, f32[256,256]{1,0:T(8,128)} %copy-done.7, f32[256,256]{1,0:T(8,128)} %copy-done.8), custom_call_target="tpu_custom_call" | custom-call | flops 32768 | bytes 131072 | tf_op jit(solution)/shard_map/sum_after/pallas_call | solution.py:98
  54.7 0.7 fusion.40
  55.4 2.2 %maximum_subtract_fusion = f32[8,1024]{1,0:T(8,128)S(1)} fusion(f32[8,256]{1,0:T(8,128)S(1)} %get-tuple-element.28, f32[8,256]{1,0:T(8,128)S(1)} %get-tuple-element.27, f32[8,256]{1,0:T(8,128)S(1)} %get-tuple-element.26, f32[8,256]{1,0:T(8,128)S(1)} %get-tuple-element.29, f32[256,256]{1,0:T(8,128)} %get-tuple-element.9, f32[256,256]{1,0:T(8,128)} %get-tuple-element.8, ...), kind=kOutput, calls=%fused_computation.51 | convolution fusion | flops 25985024 | bytes 1122304 | tf_op jit(solution)/shard_map/dot_general | solution.py:109
  57.6 5.7 %collective-permute-start.7 = (f32[8,1280]{1,0:T(8,128)S(1)}, f32[8,1280]{1,0:T(8,128)S(1)}, u32[]{:S(2)}, u32[]{:S(2)}) collective-permute-start(f32[8,1280]{1,0:T(8,128)S(1)} %pad_maximum_fusion.7), channel_id=1, source_target_pairs={{0,3},{1,2},{2,1},{3,0},{4,7},{5,6},{6,5},{7,4},{8,11},{9,10},{10,... | collective-permute-start | bytes 122888 | tf_op jit(solution)/shard_map/ppermute | solution.py:123
  63.3 0.0 collective-permute-start.8
  63.3 0.5 collective-permute-start.9
  63.8 1.2 %collective-permute-done.7 = f32[8,1280]{1,0:T(8,128)S(1)} collective-permute-done((f32[8,1280]{1,0:T(8,128)S(1)}, f32[8,1280]{1,0:T(8,128)S(1)}, u32[]{:S(2)}, u32[]{:S(2)}) %collective-permute-start.7) | collective-permute-done | bytes 40992 | tf_op jit(solution)/shard_map/ppermute | solution.py:123
  65.0 2.7 %collective-permute-done.8 = f32[8,1280]{1,0:T(8,128)S(1)} collective-permute-done((f32[8,1280]{1,0:T(8,128)S(1)}, f32[8,1280]{1,0:T(8,128)S(1)}, u32[]{:S(2)}, u32[]{:S(2)}) %collective-permute-start.8) | collective-permute-done | bytes 40992 | tf_op jit(solution)/shard_map/ppermute | solution.py:123
  67.6 0.9 %fusion.9 = f32[8,256]{1,0:T(8,128)S(1)} fusion(f32[2,256,1024]{2,1,0:T(8,128)S(1)} %copy-done.2, f32[8,1280]{1,0:T(8,128)S(1)} %collective-permute-done.7, f32[8,1280]{1,0:T(8,128)S(1)} %collective-permute-done.8, f32[8,1024]{1,0:T(8,128)S(1)} %maximum_subtract_fusion, f32[8,1280]{1,0:T(8,128)S(1)} %collective-permute-done.9), kind=kOutput, calls=%fused_computation.11 | convolution fusion | flops 25190400 | bytes 1187840 | tf_op jit(solution)/shard_map/dot_general | solution.py:109
  68.5 0.0 copy-start.11
  68.6 0.6 fusion.7
  69.2 0.9 %fusion.13 = f32[8,256]{1,0:T(8,128)S(1)} fusion(f32[2,256,1024]{2,1,0:T(8,128)S(1)} %copy-done.2, f32[8,256]{1,0:T(8,128)S(1)} %get-tuple-element.17, f32[8,256]{1,0:T(8,128)S(1)} %get-tuple-element.16, f32[8,256]{1,0:T(8,128)S(1)} %get-tuple-element.15, f32[8,256]{1,0:T(8,128)S(1)} %get-tuple-element.14), kind=kOutput, calls=%fused_computation.15 | convolution fusion | flops 25190400 | bytes 1089536 | tf_op jit(solution)/shard_map/dot_general | solution.py:109
  70.1 0.6 fusion.11
  70.8 0.1 collective-permute-start.10
  70.9 1.6 %collective-permute-start.11 = (f32[8,1280]{1,0:T(8,128)S(1)}, f32[8,1280]{1,0:T(8,128)S(1)}, u32[]{:S(2)}, u32[]{:S(2)}) collective-permute-start(f32[8,1280]{1,0:T(8,128)S(1)} %get-tuple-element.20), channel_id=1, source_target_pairs={{0,2},{1,3},{2,0},{3,1},{4,6},{5,7},{6,4},{7,5},{8,10},{9,11},{10,... | collective-permute-start | bytes 122888 | tf_op jit(solution)/shard_map/ppermute | solution.py:123
  72.4 2.1 %collective-permute-start.12 = (f32[8,1280]{1,0:T(8,128)S(1)}, f32[8,1280]{1,0:T(8,128)S(1)}, u32[]{:S(2)}, u32[]{:S(2)}) collective-permute-start(f32[8,1280]{1,0:T(8,128)S(1)} %get-tuple-element.18), channel_id=1, source_target_pairs={{0,3},{1,2},{2,1},{3,0},{4,7},{5,6},{6,5},{7,4},{8,11},{9,10},{10,... | collective-permute-start | bytes 122888 | tf_op jit(solution)/shard_map/ppermute | solution.py:123
  74.5 0.6 maximum_bitcast_fusion
  75.1 0.2 collective-permute-done.11
  75.3 2.2 %collective-permute-done.12 = f32[8,1280]{1,0:T(8,128)S(1)} collective-permute-done((f32[8,1280]{1,0:T(8,128)S(1)}, f32[8,1280]{1,0:T(8,128)S(1)}, u32[]{:S(2)}, u32[]{:S(2)}) %collective-permute-start.12) | collective-permute-done | bytes 40992 | tf_op jit(solution)/shard_map/ppermute | solution.py:123
  77.6 0.5 fusion.33
  78.1 0.6 maximum_bitcast_fusion.1
  (37 shorter events, 0.1 us)
Async XLA Ops:
  0.6 19.1 %copy-start = (f32[256,1024]{1,0:T(8,128)S(1)}, f32[256,1024]{1,0:T(8,128)}, u32[]{:S(2)}) copy-start(f32[256,1024]{1,0:T(8,128)} %param.9) | copy-start | bytes 3145732
  1.7 9.6 %collective-permute-start = (f32[256,256]{1,0:T(8,128)S(1)}, f32[256,256]{1,0:T(8,128)S(1)}, u32[]{:S(2)}, u32[]{:S(2)}) collective-permute-start(f32[256,256]{1,0:T(8,128)S(1)} %dynamic-slice_bitcast_fusion), channel_id=1, source_target_pairs={{0,18},{1,19},{2,16},{3,17},{16,2},{17,3},{18,0},{19,1},{4,22},{5,... | collective-permute-start | bytes 786440 | tf_op jit(solution)/shard_map/ppermute | solution.py:119
  5.1 13.5 %collective-permute-start.2 = (f32[256,256]{1,0:T(8,128)S(1)}, f32[256,256]{1,0:T(8,128)S(1)}, u32[]{:S(2)}, u32[]{:S(2)}) collective-permute-start(f32[256,256]{1,0:T(8,128)S(1)} %dynamic-slice_bitcast_fusion), channel_id=1, source_target_pairs={{0,1},{1,0},{2,3},{3,2},{4,5},{5,4},{6,7},{7,6},{8,9},{9,8},{10,11... | collective-permute-start | bytes 786440 | tf_op jit(solution)/shard_map/ppermute | solution.py:115
  6.2 5.2 %copy-start.1 = (f32[2,256,8]{1,2,0:T(8,128)S(1)}, f32[2,256,8]{1,2,0:T(8,128)}, u32[]{:S(2)}) copy-start(f32[2,256,8]{1,2,0:T(8,128)} %param.7) | copy-start | bytes 49156
  13.2 5.4 %collective-permute-start.1 = (f32[256,256]{1,0:T(8,128)S(1)}, f32[256,256]{1,0:T(8,128)S(1)}, u32[]{:S(2)}, u32[]{:S(2)}) collective-permute-start(f32[256,256]{1,0:T(8,128)S(1)} %get-tuple-element.5), channel_id=1, source_target_pairs={{0,1},{1,0},{2,3},{3,2},{4,5},{5,4},{6,7},{7,6},{8,9},{9,8},{10,11... | collective-permute-start | bytes 786440 | tf_op jit(solution)/shard_map/ppermute | solution.py:115
  14.5 19.8 %all-to-all-start = ((f32[8,64,512]{2,1,0:T(8,128)}), f32[8,64,512]{2,1,0:T(8,128)S(1)}, u32[]{:S(2)}, u32[]{:S(2)}) async-start(f32[8,64,512]{2,1,0:T(8,128)} %get-tuple-element.4), calls=%async_computation | async-start | bytes 2097152 | tf_op jit(solution)/shard_map/all_to_all | solution.py:167
  20.8 13.5 %copy-start.4 = (f32[256,256]{1,0:T(8,128)}, f32[256,256]{1,0:T(8,128)S(1)}, u32[]{:S(2)}) copy-start(f32[256,256]{1,0:T(8,128)S(1)} %convolution_bitcast_fusion.refs_0_) | copy-start | bytes 786436
  20.8 23.9 %collective-permute-start.3 = (f32[256,256]{1,0:T(8,128)S(1)}, f32[256,256]{1,0:T(8,128)S(1)}, u32[]{:S(2)}, u32[]{:S(2)}) collective-permute-start(f32[256,256]{1,0:T(8,128)S(1)} %convolution_bitcast_fusion.refs_0_), channel_id=1, source_target_pairs={{0,0},{32,1},{80,2},{240,3},{16,16},{48,17},{64,18},{224,19},{1,32... | collective-permute-start | bytes 786440 | tf_op jit(solution)/shard_map/ppermute | solution.py:136
  24.5 20.2 %collective-permute-start.4 = (f32[256,256]{1,0:T(8,128)S(1)}, f32[256,256]{1,0:T(8,128)S(1)}, u32[]{:S(2)}, u32[]{:S(2)}) collective-permute-start(f32[256,256]{1,0:T(8,128)S(1)} %convolution_bitcast_fusion.refs_0_), channel_id=1, source_target_pairs={{1,0},{33,1},{81,2},{241,3},{17,16},{49,17},{65,18},{225,19},{18,3... | collective-permute-start | bytes 786440 | tf_op jit(solution)/shard_map/ppermute | solution.py:136
  24.6 20.1 %collective-permute-start.5 = (f32[256,256]{1,0:T(8,128)S(1)}, f32[256,256]{1,0:T(8,128)S(1)}, u32[]{:S(2)}, u32[]{:S(2)}) collective-permute-start(f32[256,256]{1,0:T(8,128)S(1)} %convolution_bitcast_fusion.refs_0_), channel_id=1, source_target_pairs={{18,0},{50,1},{66,2},{226,3},{2,16},{34,17},{82,18},{242,19},{19,3... | collective-permute-start | bytes 786440 | tf_op jit(solution)/shard_map/ppermute | solution.py:136
  31.1 13.7 %collective-permute-start.6 = (f32[256,256]{1,0:T(8,128)S(1)}, f32[256,256]{1,0:T(8,128)S(1)}, u32[]{:S(2)}, u32[]{:S(2)}) collective-permute-start(f32[256,256]{1,0:T(8,128)S(1)} %convolution_bitcast_fusion.refs_0_), channel_id=1, source_target_pairs={{19,0},{51,1},{67,2},{227,3},{3,16},{35,17},{83,18},{243,19},{0,32... | collective-permute-start | bytes 786440 | tf_op jit(solution)/shard_map/ppermute | solution.py:136
  34.3 1.0 %copy-start.3 = (f32[8,64,512]{2,1,0:T(8,128)}, f32[8,64,512]{2,1,0:T(8,128)S(1)}, u32[]{:S(2)}) copy-start(f32[8,64,512]{2,1,0:T(8,128)S(1)} %all-to-all-done.parts_ref) | copy-start | bytes 3145732
  37.2 15.3 %all-to-all-start.1 = ((f32[8,8,512]{2,1,0:T(8,128)}), f32[8,8,512]{2,1,0:T(8,128)S(1)}, u32[]{:S(2)}, u32[]{:S(2)}) async-start(f32[8,8,512]{2,1,0:T(8,128)} %bitcast.35), calls=%async_computation.1 | async-start | bytes 262144 | tf_op jit(solution)/shard_map/all_to_all | solution.py:172
  44.7 7.8 %copy-start.5 = (f32[256,256]{1,0:T(8,128)}, f32[256,256]{1,0:T(8,128)S(1)}, u32[]{:S(2)}) copy-start(f32[256,256]{1,0:T(8,128)S(1)} %collective-permute-done.3.refs_0_) | copy-start | bytes 786436
  44.7 0.8 copy-start.6
  44.8 0.8 %copy-start.7 = (f32[256,256]{1,0:T(8,128)}, f32[256,256]{1,0:T(8,128)S(1)}, u32[]{:S(2)}) copy-start(f32[256,256]{1,0:T(8,128)S(1)} %collective-permute-done.5.refs_2_) | copy-start | bytes 786436
  45.6 0.7 copy-start.8
  47.4 20.2 %copy-start.2 = (f32[2,256,1024]{2,1,0:T(8,128)S(1)}, f32[2,256,1024]{2,1,0:T(8,128)}, u32[]{:S(2)}) copy-start(f32[2,256,1024]{2,1,0:T(8,128)} %param.8) | copy-start | bytes 6291460
  52.5 0.7 copy-start.9
  55.4 13.8 %copy-start.14 = (f32[8,512]{1,0:T(8,128)S(1)}, f32[8,512]{1,0:T(8,128)}, u32[]{:S(2)}) copy-start(f32[8,512]{1,0:T(8,128)} %sum_after.3) | copy-start | bytes 49156
  57.6 7.4 %collective-permute-start.7 = (f32[8,1280]{1,0:T(8,128)S(1)}, f32[8,1280]{1,0:T(8,128)S(1)}, u32[]{:S(2)}, u32[]{:S(2)}) collective-permute-start(f32[8,1280]{1,0:T(8,128)S(1)} %pad_maximum_fusion.7), channel_id=1, source_target_pairs={{0,3},{1,2},{2,1},{3,0},{4,7},{5,6},{6,5},{7,4},{8,11},{9,10},{10,... | collective-permute-start | bytes 122888 | tf_op jit(solution)/shard_map/ppermute | solution.py:123
  63.3 4.4 %collective-permute-start.8 = (f32[8,1280]{1,0:T(8,128)S(1)}, f32[8,1280]{1,0:T(8,128)S(1)}, u32[]{:S(2)}, u32[]{:S(2)}) collective-permute-start(f32[8,1280]{1,0:T(8,128)S(1)} %pad_maximum_fusion.7), channel_id=1, source_target_pairs={{0,2},{1,3},{2,0},{3,1},{4,6},{5,7},{6,4},{7,5},{8,10},{9,11},{10,... | collective-permute-start | bytes 122888 | tf_op jit(solution)/shard_map/ppermute | solution.py:123
  63.3 4.4 %collective-permute-start.9 = (f32[8,1280]{1,0:T(8,128)S(1)}, f32[8,1280]{1,0:T(8,128)S(1)}, u32[]{:S(2)}, u32[]{:S(2)}) collective-permute-start(f32[8,1280]{1,0:T(8,128)S(1)} %pad_maximum_fusion.7), channel_id=1, source_target_pairs={{0,1},{1,0},{2,3},{3,2},{4,5},{5,4},{6,7},{7,6},{8,9},{9,8},{10,11... | collective-permute-start | bytes 122888 | tf_op jit(solution)/shard_map/ppermute | solution.py:123
  68.5 9.0 %copy-start.10 = (f32[256,256]{1,0:T(8,128)S(1)}, f32[256,256]{1,0:T(8,128)}, u32[]{:S(2)}) copy-start(f32[256,256]{1,0:T(8,128)} %get-tuple-element.6) | copy-start | bytes 786436
  68.5 9.0 %copy-start.11 = (f32[256,256]{1,0:T(8,128)S(1)}, f32[256,256]{1,0:T(8,128)}, u32[]{:S(2)}) copy-start(f32[256,256]{1,0:T(8,128)} %get-tuple-element.7) | copy-start | bytes 786436
  68.6 9.0 %copy-start.12 = (f32[256,256]{1,0:T(8,128)S(1)}, f32[256,256]{1,0:T(8,128)}, u32[]{:S(2)}) copy-start(f32[256,256]{1,0:T(8,128)} %get-tuple-element.8) | copy-start | bytes 786436
  68.6 9.0 %copy-start.13 = (f32[256,256]{1,0:T(8,128)S(1)}, f32[256,256]{1,0:T(8,128)}, u32[]{:S(2)}) copy-start(f32[256,256]{1,0:T(8,128)} %get-tuple-element.9) | copy-start | bytes 786436
  70.8 4.3 %collective-permute-start.10 = (f32[8,1280]{1,0:T(8,128)S(1)}, f32[8,1280]{1,0:T(8,128)S(1)}, u32[]{:S(2)}, u32[]{:S(2)}) collective-permute-start(f32[8,1280]{1,0:T(8,128)S(1)} %get-tuple-element.19), channel_id=1, source_target_pairs={{0,1},{1,0},{2,3},{3,2},{4,5},{5,4},{6,7},{7,6},{8,9},{9,8},{10,11... | collective-permute-start | bytes 122888 | tf_op jit(solution)/shard_map/ppermute | solution.py:123
  70.9 4.4 %collective-permute-start.11 = (f32[8,1280]{1,0:T(8,128)S(1)}, f32[8,1280]{1,0:T(8,128)S(1)}, u32[]{:S(2)}, u32[]{:S(2)}) collective-permute-start(f32[8,1280]{1,0:T(8,128)S(1)} %get-tuple-element.20), channel_id=1, source_target_pairs={{0,2},{1,3},{2,0},{3,1},{4,6},{5,7},{6,4},{7,5},{8,10},{9,11},{10,... | collective-permute-start | bytes 122888 | tf_op jit(solution)/shard_map/ppermute | solution.py:123
  72.4 5.0 %collective-permute-start.12 = (f32[8,1280]{1,0:T(8,128)S(1)}, f32[8,1280]{1,0:T(8,128)S(1)}, u32[]{:S(2)}, u32[]{:S(2)}) collective-permute-start(f32[8,1280]{1,0:T(8,128)S(1)} %get-tuple-element.18), channel_id=1, source_target_pairs={{0,3},{1,2},{2,1},{3,0},{4,7},{5,6},{6,5},{7,4},{8,11},{9,10},{10,... | collective-permute-start | bytes 122888 | tf_op jit(solution)/shard_map/ppermute | solution.py:123

commit v3 on v2

--- a/solution.py
+++ b/solution.py
@@ -18,7 +18,9 @@
     return high, (block - high.astype(jnp.float32)).astype(jnp.bfloat16)
 
 
-def product_kernel(factor_hbm, solved_hbm, out_ref, factor_ref, solved_ref, sem):
+def product_kernel(at_ref, factor_hbm, solved_hbm, inverse_hbm, out_ref, slab_ref, factor_ref, solved_ref, sem, slab_sem):
+    span = pl.ds(pl.multiple_of(at_ref[2] * 256, 256), 256)
+    slab = pltpu.make_async_copy(inverse_hbm.at[0, :, span], slab_ref, slab_sem)
     copies = []
     for k in range(STEPS):
         span = pl.ds(k * DEPTH, DEPTH)
@@ -40,30 +42,32 @@
             preferred_element_type=jnp.float32,
         )
         if k == 0:
+            slab.start()
             out_ref[...] = term
         else:
             out_ref[...] += term
-
-
-def product(flat, solved_rows):
+    slab.wait()
+
+
+def product(at, flat, solved_rows, inverse):
     return pl.pallas_call(
         product_kernel,
-        in_specs=[pl.BlockSpec(memory_space=pl.ANY)] * 2,
-        out_specs=pl.BlockSpec(memory_space=pltpu.VMEM),
-        out_shape=pltpu.VMEM((512, 512), jnp.float32),
+        in_specs=[pl.BlockSpec(memory_space=pltpu.SMEM)] + [pl.BlockSpec(memory_space=pl.ANY)] * 3,
+        out_specs=[pl.BlockSpec(memory_space=pltpu.VMEM)] * 2,
+        out_shape=[pltpu.VMEM((512, 512), jnp.float32), jax.ShapeDtypeStruct((256, 256), jnp.float32)],
         scratch_shapes=[
             pltpu.VMEM((512, 2048), jnp.float32),
             pltpu.VMEM((2048, 512), jnp.float32),
             pltpu.SemaphoreType.DMA((2, STEPS)),
+            pltpu.SemaphoreType.DMA,
         ],
         compiler_params=pltpu.CompilerParams(vmem_limit_bytes=20 << 20),
         cost_estimate=pl.CostEstimate(flops=6 * 512 * 512 * 2048, bytes_accessed=9 << 20, transcendentals=0),
         name="product",
-    )(pltpu.with_memory_space_constraint(flat, pltpu.HBM), pltpu.with_memory_space_constraint(solved_rows, pltpu.HBM))
-
-
-def place_kernel(at_ref, update_ref, right_ref, slab_ref, out_ref, copy_ref):
-    copy_ref[...] = slab_ref[...]
+    )(at, *(pltpu.with_memory_space_constraint(x, pltpu.HBM) for x in (flat, solved_rows, inverse)))
+
+
+def place_kernel(at_ref, update_ref, right_ref, out_ref):
     turned = -update_ref[...].T
     for z in range(8):
         for p in range(8):
@@ -73,42 +77,67 @@
     out_ref[at_ref[0], rows, 256:512] += right_ref[1]
 
 
-def place(at, update, right, slab):
+def place(at, update, right):
     vmem = pl.BlockSpec(memory_space=pltpu.VMEM)
     return pl.pallas_call(
         place_kernel,
-        in_specs=[pl.BlockSpec(memory_space=pltpu.SMEM), vmem, vmem, vmem],
-        out_specs=[vmem, vmem],
-        out_shape=[jax.ShapeDtypeStruct((8, 64, 512), jnp.float32), jax.ShapeDtypeStruct(slab.shape, jnp.float32)],
+        in_specs=[pl.BlockSpec(memory_space=pltpu.SMEM), vmem, vmem],
+        out_specs=vmem,
+        out_shape=jax.ShapeDtypeStruct((8, 64, 512), jnp.float32),
         compiler_params=pltpu.CompilerParams(vmem_limit_bytes=8 << 20),
         cost_estimate=pl.CostEstimate(flops=1 << 18, bytes_accessed=2 << 20, transcendentals=0),
         name="place",
-    )(at, update, right, slab)
-
-
-def sum_after(parts, awaited):
+    )(at, update, right)
+
+
+def sum_kernel(parts_ref, out_ref):
+    total = parts_ref[0]
+    for k in range(1, 8):
+        total = total + parts_ref[k]
+    out_ref[...] = total
+
+
+def sum_parts(parts):
     vmem = pl.BlockSpec(memory_space=pltpu.VMEM)
-
-    def kernel(parts_ref, *refs):
-        total = parts_ref[0]
-        for k in range(1, 8):
-            total = total + parts_ref[k]
-        refs[-1][...] = total
-
-    return pl.pallas_call(
-        kernel,
-        in_specs=[vmem] + [pl.BlockSpec(memory_space=pl.ANY)] * len(awaited),
+    return pl.pallas_call(
+        sum_kernel,
+        in_specs=[vmem],
         out_specs=vmem,
         out_shape=jax.ShapeDtypeStruct(parts.shape[1:], jnp.float32),
-        cost_estimate=pl.CostEstimate(flops=1 << 15, bytes_accessed=1 << 17, transcendentals=0),
-        name="sum_after",
-    )(parts, *awaited)
+        compiler_params=pltpu.CompilerParams(vmem_limit_bytes=8 << 20),
+        cost_estimate=pl.CostEstimate(flops=1 << 18, bytes_accessed=1 << 20, transcendentals=0),
+        name="sum_parts",
+    )(parts)
+
+
+def after(block, awaited):
+    return lax.optimization_barrier((block, awaited))[0]
 
 
 def exact(left, right, dims):
     return lax.dot_general(
         left, right, (dims, ((), ())), preferred_element_type=jnp.float32, precision=lax.Precision.HIGHEST
     )
+
+
+def block_product(at, left, pieces, name):
+    vmem = pl.BlockSpec(memory_space=pltpu.VMEM)
+
+    def kernel(at_ref, left_ref, p0, p1, p2, p3, out_ref, whole_ref):
+        for flip, piece in enumerate((p0, p1, p2, p3)):
+            whole_ref[pl.ds(pl.multiple_of((at_ref[3] ^ flip) * 256, 256), 256), :] = piece[...]
+        out_ref[...] = exact(left_ref[...], whole_ref[...], ((1,), (0,)))
+
+    return pl.pallas_call(
+        kernel,
+        in_specs=[pl.BlockSpec(memory_space=pltpu.SMEM)] + [vmem] * 5,
+        out_specs=vmem,
+        out_shape=jax.ShapeDtypeStruct((256, 256), jnp.float32),
+        scratch_shapes=[pltpu.VMEM((1024, 256), jnp.float32)],
+        compiler_params=pltpu.CompilerParams(vmem_limit_bytes=16 << 20),
+        cost_estimate=pl.CostEstimate(flops=1 << 10, bytes_accessed=1 << 10, transcendentals=0),
+        name=name,
+    )(at, left, *pieces)
 
 
 def near(block):
@@ -158,23 +187,25 @@
 def shards(factor_rows, solved_rows, right_side, inverse, coupling):
     mine = lax.axis_index(COL)
     quad = lax.axis_index("z") % 4
-    at = jnp.stack([lax.axis_index(("xl", "y")), lax.axis_index("z")])
-
-    slab = lax.dynamic_slice(inverse, (0, 0, quad * 256), (1, 256, 256))[0]
+    at = jnp.stack([lax.axis_index(("xl", "y")), lax.axis_index("z"), quad, mine])
+
+    update, slab = product(at, factor_rows.reshape(512, 2048), solved_rows, inverse)
     slab_far = far(slab)
-    update = product(factor_rows.reshape(512, 2048), solved_rows)
-    part, slab_far = place(at, update, right_side.transpose(0, 2, 1), slab_far)
+    part = place(at, update, right_side.transpose(0, 2, 1))
+    slab_far = after(slab_far, part)
     part = lax.all_to_all(part, ("xl", "y"), 0, 0, tiled=True)
-    whole = jnp.concatenate(in_order([slab, near(slab), slab_far, near(slab_far)], mine), axis=0)
-    middle = exact(coupling, whole, ((1,), (0,)))
-    part = sum_after(part, [middle])
+    beyond = jnp.concatenate([near(slab_far[64 * k : 64 * k + 64]) for k in range(4)], axis=0)
+    middle = block_product(at, coupling, [slab, near(slab), slab_far, beyond], "middle")
+    part = after(sum_parts(part), middle)
     columns = [from_quad(middle, k) for k in range(4)]
     part = lax.all_to_all(part.reshape(8, 8, 512), "z", 0, 0, tiled=True)
-    r = sum_after(part, columns)
-    columns = jnp.concatenate(turned(columns, quad), axis=0)
+    r = after(part.sum(0), columns)
+    columns = turned(columns, quad)
+    rows = jnp.concatenate([c.T for c in columns], axis=1)
+    columns = jnp.concatenate(columns, axis=0)
 
     r0, r1 = r[:, :256], r[:, 256:]
-    s = jnp.concatenate([jnp.where(mine == k, r1, 0.0) for k in range(4)], axis=1) - exact(r0, columns, ((1,), (1,)))
+    s = jnp.concatenate([jnp.where(mine == k, r1, 0.0) for k in range(4)], axis=1) - exact(r0, rows, ((1,), (0,)))
     sent = jnp.concatenate([r0, s], axis=1)
     got = [sent] + [from_col(sent, k) for k in (1, 2, 3)]
     f0 = exact(jnp.concatenate(in_order([g[:, :256] for g in got], mine), axis=1), inverse[0], ((1,), (1,)))

time: 79.1 us -> 69.9 us (0.88)
  starting transfers between devices: 40.7 us -> 35.6 us
  waiting for transfers between devices: 11.3 us -> 16 us
  local copies, waits for them, and re-layouts: 4.28 us -> 0.05 us
  matrix products: 6.81 us -> 4.56 us
  other arithmetic: 4.21 us -> 2.58 us
    ppermute x4, waiting for transfers between devices: 0.01 us -> 3.58 us  [from_quad(): return lax.ppermute(block, ('z', 'xl', 'xh', 'core'), pairs)]
    unnamed x30 -> x6, local copies, waits for them, and re-layouts: 3.21 us -> 0.01 us
    all_to_all x1, starting transfers between devices: 7.53 us -> 5 us  [shards(): part = lax.all_to_all(part.reshape(8, 8, 512), 'z', 0, 0, tiled=True)]
    dot_general x7 -> x6, matrix products: 6.81 us -> 4.56 us  [exact(): lax.dot_general(left, right, (dims, ((), ())), preferred_element_type=jnp...]
    ppermute x6, starting transfers between devices: 9.91 us -> 7.86 us  [from_col(): return lax.ppermute(block, COL, [(s, s ^ flip) for s in range(4)])]
    squeeze x1 -> x0, local copies, waits for them, and re-layouts: 1.06 us -> none  [shards(): slab = lax.dynamic_slice(inverse, (0, 0, quad * 256), (1, 256, 256))[0]]
    select_n x2 -> x1, other arithmetic: 1.06 us -> 0.01 us  [in_order(): return [jnp.where(high == 1, a[k ^ 2], a[k]) for k in range(4)]]
    ppermute x2 -> x5, waiting for transfers between devices: 0.01 us -> 0.9 us  [near(): return lax.ppermute(block, 'core', [(0, 1), (1, 0)])]
  transfers between devices with their start and end apart: 15 -> 18, of which waited for: 5 -> 10; matrix products, arithmetic and copies ran while one was open for 5% -> 3% of each run, Pallas kernels for 11% -> 6%
where the time goes in v3:
time: 69.9 us; the launch traced here: 69.6 us
  starting transfers between devices  35.6 us (51%)
  waiting for transfers between devices  16 us (23%)
  Pallas kernels  10 us (14%)
  matrix products  4.56 us (7%)
  other arithmetic  2.58 us (4%)
  between operations  0.81 us (1%)
    ppermute x4, starting transfers between devices, from_quad(): return lax.ppermute(block, ('z', 'xl', 'xh', 'core'), pairs)  12.7 us
    ppermute x6, starting transfers between devices, from_col(): return lax.ppermute(block, COL, [(s, s ^ flip) for s in range(4)])  7.86 us
    ppermute x6, waiting for transfers between devices, from_col(): return lax.ppermute(block, COL, [(s, s ^ flip) for s in range(4)])  6.31 us
    pallas_call x1, Pallas kernels, product(): pl.pallas_call(product_kernel, in_specs=[pl.BlockSpec(memory_space=pltpu....  5.73 us
    all_to_all x1, waiting for transfers between devices, shards(): part = lax.all_to_all(part.reshape(8, 8, 512), 'z', 0, 0, tiled=True)  5.18 us
    all_to_all x1, starting transfers between devices, shards(): part = lax.all_to_all(part.reshape(8, 8, 512), 'z', 0, 0, tiled=True)  5 us
    dot_general x6, matrix products, exact(): lax.dot_general(left, right, (dims, ((), ())), preferred_element_type=jnp...  4.56 us
    all_to_all x1, starting transfers between devices, shards(): part = lax.all_to_all(part, ('xl', 'y'), 0, 0, tiled=True)  4.32 us
  transfers between devices with their start and end apart: 18, of which 10 were waited for; matrix products, arithmetic and copies ran while one was open for 3% of the time, Pallas kernels for 6%

profile of v3, /device:TPU:1, one launch (start us, length us, event | category | flops | bytes accessed | tf_op | source)
XLA Modules:
  0.0 69.6 jit_solution(14144012700433246145)
XLA Ops:
  0.6 0.1 pad_add_fusion.at_ref
  0.7 5.7 %product.1 = (f32[512,512]{1,0:T(8,128)S(1)}, f32[256,256]{1,0:T(8,128)S(1)}) custom-call(s32[4]{0:T(128)S(1)} %pad_add_fusion.at_ref, f32[512,2048]{1,0:T(8,128)} %bitcast.40, f32[2048,512]{1,0:T(8,128)} %solved_hbm.1, f32[2,256,1024]{2,1,0:T(8,128)} %inverse_hbm.1), custom_call_target="tpu_custom_call" | custom-call | flops 3221225472 | bytes 9437184 | tf_op jit(solution)/shard_map/product/pallas_call | solution.py:53
  6.5 3.4 %collective-permute-start.1 = (f32[256,256]{1,0:T(8,128)S(1)}, f32[256,256]{1,0:T(8,128)S(1)}, u32[]{:S(2)}, u32[]{:S(2)}) collective-permute-start(f32[256,256]{1,0:T(8,128)S(1)} %get-tuple-element.8.p0), channel_id=1, source_target_pairs={{0,18},{1,19},{2,16},{3,17},{16,2},{17,3},{18,0},{19,1},{4,22},{5,... | collective-permute-start | bytes 786440 | tf_op jit(solution)/shard_map/ppermute | solution.py:148
  9.9 1.9 %place.1 = f32[8,64,512]{2,1,0:T(8,128)} custom-call(s32[4]{0:T(128)S(1)} %pad_add_fusion.at_ref, f32[512,512]{1,0:T(8,128)S(1)} %get-tuple-element.7.update_ref, f32[2,8,256]{2,1,0:T(8,128)S(1)} %bitcast.33), custom_call_target="tpu_custom_call" | custom-call | flops 262144 | bytes 2097152 | tf_op jit(solution)/shard_map/place/pallas_call | solution.py:82
  11.8 4.3 %all-to-all-start = ((f32[8,64,512]{2,1,0:T(8,128)}), f32[8,64,512]{2,1,0:T(8,128)S(1)}, u32[]{:S(2)}, u32[]{:S(2)}) async-start(f32[8,64,512]{2,1,0:T(8,128)} %place.1), calls=%async_computation | async-start | bytes 2097152 | tf_op jit(solution)/shard_map/all_to_all | solution.py:196
  16.1 1.2 %collective-permute-start = (f32[256,256]{1,0:T(8,128)S(1)}, f32[256,256]{1,0:T(8,128)S(1)}, u32[]{:S(2)}, u32[]{:S(2)}) collective-permute-start(f32[256,256]{1,0:T(8,128)S(1)} %get-tuple-element.8.p0), channel_id=1, source_target_pairs={{0,1},{1,0},{2,3},{3,2},{4,5},{5,4},{6,7},{7,6},{8,9},{9,8},{10,11... | collective-permute-start | bytes 786440 | tf_op jit(solution)/shard_map/ppermute | solution.py:144
  17.3 0.0 collective-permute-done.1.p2
  17.3 0.1 collective-permute-start.2
  17.5 0.4 collective-permute-start.3
  17.9 0.1 collective-permute-start.4
  18.0 0.4 collective-permute-start.5
  18.4 0.2 collective-permute-done.2
  18.7 0.2 collective-permute-done.3
  18.8 0.4 collective-permute-done.4
  19.2 0.2 collective-permute-done.5
  19.4 0.0 collective-permute-done.p1
  19.4 1.7 %middle.1 = f32[256,256]{1,0:T(8,128)S(1)} custom-call(s32[4]{0:T(128)S(1)} %pad_add_fusion.at_ref, f32[256,1024]{1,0:T(8,128)S(1)} %copy-done, f32[256,256]{1,0:T(8,128)S(1)} %get-tuple-element.8.p0, f32[256,256]{1,0:T(8,128)S(1)} %collective-permute-done.p1, f32[256,256]{1,0:T(8,128)S(1)} %collective-permute-done.1.p2, f32[256,256]{1,0:T(8,128)S(1)} %pad_maximum_fusion.p3), custom_call_target="tpu_custom_call" | custom-call | flops 1024 | bytes 1024 | tf_op jit(solution)/shard_map/middle/pallas_call | solution.py:131
  21.1 3.8 %collective-permute-start.6 = (f32[256,256]{1,0:T(8,128)S(1)}, f32[256,256]{1,0:T(8,128)S(1)}, u32[]{:S(2)}, u32[]{:S(2)}) collective-permute-start(f32[256,256]{1,0:T(8,128)S(1)} %middle.1), channel_id=1, source_target_pairs={{0,0},{32,1},{80,2},{240,3},{16,16},{48,17},{64,18},{224,19},{1,32... | collective-permute-start | bytes 786440 | tf_op jit(solution)/shard_map/ppermute | solution.py:165
  24.9 0.1 collective-permute-start.7
  25.0 5.0 %collective-permute-start.8 = (f32[256,256]{1,0:T(8,128)S(1)}, f32[256,256]{1,0:T(8,128)}, u32[]{:S(2)}, u32[]{:S(2)}) collective-permute-start(f32[256,256]{1,0:T(8,128)S(1)} %middle.1), channel_id=1, source_target_pairs={{18,0},{50,1},{66,2},{226,3},{2,16},{34,17},{82,18},{242,19},{19,3... | collective-permute-start | bytes 786440 | tf_op jit(solution)/shard_map/ppermute | solution.py:165
  30.1 3.8 %collective-permute-start.9 = (f32[256,256]{1,0:T(8,128)S(1)}, f32[256,256]{1,0:T(8,128)}, u32[]{:S(2)}, u32[]{:S(2)}) collective-permute-start(f32[256,256]{1,0:T(8,128)S(1)} %middle.1), channel_id=1, source_target_pairs={{19,0},{51,1},{67,2},{227,3},{3,16},{35,17},{83,18},{243,19},{0,32... | collective-permute-start | bytes 786440 | tf_op jit(solution)/shard_map/ppermute | solution.py:165
  33.8 0.0 all-to-all-done.parts_ref
  33.8 0.7 %sum_parts.1 = f32[64,512]{1,0:T(8,128)} custom-call(f32[8,64,512]{2,1,0:T(8,128)S(1)} %all-to-all-done.parts_ref), custom_call_target="tpu_custom_call" | custom-call | flops 262144 | bytes 1048576 | tf_op jit(solution)/shard_map/sum_parts/pallas_call | solution.py:102
  34.5 5.0 %all-to-all-start.1 = ((f32[8,8,512]{2,1,0:T(8,128)}), f32[8,8,512]{2,1,0:T(8,128)S(1)}, u32[]{:S(2)}, u32[]{:S(2)}) async-start(f32[8,8,512]{2,1,0:T(8,128)} %bitcast.6), calls=%async_computation.1 | async-start | bytes 262144 | tf_op jit(solution)/shard_map/all_to_all | solution.py:201
  39.6 0.0 collective-permute-done.6
  39.6 0.0 collective-permute-done.7
  39.6 0.0 collective-permute-done.8
  39.6 3.6 %collective-permute-done.9 = f32[256,256]{1,0:T(8,128)} collective-permute-done((f32[256,256]{1,0:T(8,128)S(1)}, f32[256,256]{1,0:T(8,128)}, u32[]{:S(2)}, u32[]{:S(2)}) %collective-permute-start.9) | collective-permute-done | bytes 262176 | tf_op jit(solution)/shard_map/ppermute | solution.py:165
  43.2 1.2 %broadcast_select_fusion.7 = (f32[256,256]{1,0:T(8,128)S(1)}, f32[256,256]{1,0:T(8,128)S(1)}, f32[256,256]{1,0:T(8,128)S(1)}, f32[256,256]{1,0:T(8,128)S(1)}) fusion(pred[]{:T(512)S(6)} %eq.49, f32[256,256]{1,0:T(8,128)} %collective-permute-done.7, f32[256,256]{1,0:T(8,128)} %collective-permute-done.8, pred[]{:T(512)S(6)} %eq.50, ...), kind=kLoop, calls=%fused_computation.36 | loop fusion | flops 524288 | bytes 2097154 | tf_op jit(solution)/shard_map/jit(_where)/select_n | solution.py:176
  44.4 5.2 %all-to-all-done.1 = f32[8,8,512]{2,1,0:T(8,128)S(1)} async-done(((f32[8,8,512]{2,1,0:T(8,128)}), f32[8,8,512]{2,1,0:T(8,128)S(1)}, u32[]{:S(2)}, u32[]{:S(2)}) %all-to-all-start.1) | async-done | bytes 131104 | tf_op jit(solution)/shard_map/all_to_all | solution.py:201
  49.6 1.0 %convolution_subtract_fusion = f32[8,1024]{1,0:T(8,128)S(1)} fusion(f32[256,256]{0,1:T(8,128)S(1)} %bitcast.37, f32[256,256]{0,1:T(8,128)S(1)} %bitcast.36, f32[256,256]{0,1:T(8,128)S(1)} %bitcast.35, f32[256,256]{0,1:T(8,128)S(1)} %bitcast.34, f32[8,256]{1,0:T(8,128)S(1)} %get-tuple-element.34, f32[8,256]{1,0:T(8,128)S(1)} %get-tuple-element.33, ...), kind=kOutput, calls=%fused_computation | convolution fusion | flops 25985024 | bytes 1122304 | tf_op jit(solution)/shard_map/dot_general | solution.py:118
  50.6 1.2 %collective-permute-start.10 = (f32[8,1280]{1,0:T(8,128)S(1)}, f32[8,1280]{1,0:T(8,128)S(1)}, u32[]{:S(2)}, u32[]{:S(2)}) collective-permute-start(f32[8,1280]{1,0:T(8,128)S(1)} %pad_maximum_fusion.5), channel_id=1, source_target_pairs={{0,3},{1,2},{2,1},{3,0},{4,7},{5,6},{6,5},{7,4},{8,11},{9,10},{10,... | collective-permute-start | bytes 122888 | tf_op jit(solution)/shard_map/ppermute | solution.py:152
  51.8 2.9 %collective-permute-start.11 = (f32[8,1280]{1,0:T(8,128)S(1)}, f32[8,1280]{1,0:T(8,128)S(1)}, u32[]{:S(2)}, u32[]{:S(2)}) collective-permute-start(f32[8,1280]{1,0:T(8,128)S(1)} %pad_maximum_fusion.5), channel_id=1, source_target_pairs={{0,2},{1,3},{2,0},{3,1},{4,6},{5,7},{6,4},{7,5},{8,10},{9,11},{10,... | collective-permute-start | bytes 122888 | tf_op jit(solution)/shard_map/ppermute | solution.py:152
  54.7 0.0 collective-permute-start.12
  54.7 1.5 %collective-permute-done.10 = f32[8,1280]{1,0:T(8,128)S(1)} collective-permute-done((f32[8,1280]{1,0:T(8,128)S(1)}, f32[8,1280]{1,0:T(8,128)S(1)}, u32[]{:S(2)}, u32[]{:S(2)}) %collective-permute-start.10) | collective-permute-done | bytes 40992 | tf_op jit(solution)/shard_map/ppermute | solution.py:152
  56.2 1.1 %collective-permute-done.11 = f32[8,1280]{1,0:T(8,128)S(1)} collective-permute-done((f32[8,1280]{1,0:T(8,128)S(1)}, f32[8,1280]{1,0:T(8,128)S(1)}, u32[]{:S(2)}, u32[]{:S(2)}) %collective-permute-start.11) | collective-permute-done | bytes 40992 | tf_op jit(solution)/shard_map/ppermute | solution.py:152
  57.3 0.9 %fusion.21 = f32[8,256]{1,0:T(8,128)S(1)} fusion(f32[2,256,1024]{2,1,0:T(8,128)S(1)} %copy-done.2, f32[8,256]{1,0:T(8,128)S(1)} %get-tuple-element.23, f32[8,256]{1,0:T(8,128)S(1)} %get-tuple-element.22, f32[8,256]{1,0:T(8,128)S(1)} %get-tuple-element.21, f32[8,256]{1,0:T(8,128)S(1)} %get-tuple-element.20), kind=kOutput, calls=%fused_computation.22 | convolution fusion | flops 25190400 | bytes 1089536 | tf_op jit(solution)/shard_map/dot_general | solution.py:118
  58.2 0.6 fusion.19
  58.9 0.9 %fusion.17 = f32[8,256]{1,0:T(8,128)S(1)} fusion(f32[2,256,1024]{2,1,0:T(8,128)S(1)} %copy-done.2, f32[8,1280]{1,0:T(8,128)S(1)} %collective-permute-done.10, f32[8,1280]{1,0:T(8,128)S(1)} %collective-permute-done.11, f32[8,1024]{1,0:T(8,128)S(1)} %convolution_subtract_fusion, f32[8,1280]{1,0:T(8,128)S(1)} %collective-permute-done.12), kind=kOutput, calls=%fused_computation.18 | convolution fusion | flops 25190400 | bytes 1187840 | tf_op jit(solution)/shard_map/dot_general | solution.py:118
  59.8 0.6 fusion.15
  60.4 0.5 collective-permute-start.13
  61.0 2.4 %collective-permute-start.14 = (f32[8,1280]{1,0:T(8,128)S(1)}, f32[8,1280]{1,0:T(8,128)S(1)}, u32[]{:S(2)}, u32[]{:S(2)}) collective-permute-start(f32[8,1280]{1,0:T(8,128)S(1)} %get-tuple-element.26), channel_id=1, source_target_pairs={{0,2},{1,3},{2,0},{3,1},{4,6},{5,7},{6,4},{7,5},{8,10},{9,11},{10,... | collective-permute-start | bytes 122888 | tf_op jit(solution)/shard_map/ppermute | solution.py:152
  63.3 0.9 %collective-permute-start.15 = (f32[8,1280]{1,0:T(8,128)S(1)}, f32[8,1280]{1,0:T(8,128)S(1)}, u32[]{:S(2)}, u32[]{:S(2)}) collective-permute-start(f32[8,1280]{1,0:T(8,128)S(1)} %get-tuple-element.24), channel_id=1, source_target_pairs={{0,3},{1,2},{2,1},{3,0},{4,7},{5,6},{6,5},{7,4},{8,11},{9,10},{10,... | collective-permute-start | bytes 122888 | tf_op jit(solution)/shard_map/ppermute | solution.py:152
  64.2 0.6 maximum_bitcast_fusion
  64.8 0.5 collective-permute-done.14
  65.3 3.1 %collective-permute-done.15 = f32[8,1280]{1,0:T(8,128)S(1)} collective-permute-done((f32[8,1280]{1,0:T(8,128)S(1)}, f32[8,1280]{1,0:T(8,128)S(1)}, u32[]{:S(2)}, u32[]{:S(2)}) %collective-permute-start.15) | collective-permute-done | bytes 40992 | tf_op jit(solution)/shard_map/ppermute | solution.py:152
  68.5 0.5 fusion.39
  69.0 0.6 maximum_bitcast_fusion.1
  (19 shorter events, 0.1 us)
Async XLA Ops:
  0.7 9.1 %copy-start.1 = (f32[2,256,8]{1,2,0:T(8,128)S(1)}, f32[2,256,8]{1,2,0:T(8,128)}, u32[]{:S(2)}) copy-start(f32[2,256,8]{1,2,0:T(8,128)} %param.7) | copy-start | bytes 49156
  6.5 10.8 %collective-permute-start.1 = (f32[256,256]{1,0:T(8,128)S(1)}, f32[256,256]{1,0:T(8,128)S(1)}, u32[]{:S(2)}, u32[]{:S(2)}) collective-permute-start(f32[256,256]{1,0:T(8,128)S(1)} %get-tuple-element.8.p0), channel_id=1, source_target_pairs={{0,18},{1,19},{2,16},{3,17},{16,2},{17,3},{18,0},{19,1},{4,22},{5,... | collective-permute-start | bytes 786440 | tf_op jit(solution)/shard_map/ppermute | solution.py:148
  11.7 7.6 %copy-start = (f32[256,1024]{1,0:T(8,128)S(1)}, f32[256,1024]{1,0:T(8,128)}, u32[]{:S(2)}) copy-start(f32[256,1024]{1,0:T(8,128)} %left_ref.1) | copy-start | bytes 3145732
  11.8 22.1 %all-to-all-start = ((f32[8,64,512]{2,1,0:T(8,128)}), f32[8,64,512]{2,1,0:T(8,128)S(1)}, u32[]{:S(2)}, u32[]{:S(2)}) async-start(f32[8,64,512]{2,1,0:T(8,128)} %place.1), calls=%async_computation | async-start | bytes 2097152 | tf_op jit(solution)/shard_map/all_to_all | solution.py:196
  16.1 3.3 %collective-permute-start = (f32[256,256]{1,0:T(8,128)S(1)}, f32[256,256]{1,0:T(8,128)S(1)}, u32[]{:S(2)}, u32[]{:S(2)}) collective-permute-start(f32[256,256]{1,0:T(8,128)S(1)} %get-tuple-element.8.p0), channel_id=1, source_target_pairs={{0,1},{1,0},{2,3},{3,2},{4,5},{5,4},{6,7},{7,6},{8,9},{9,8},{10,11... | collective-permute-start | bytes 786440 | tf_op jit(solution)/shard_map/ppermute | solution.py:144
  17.3 1.3 %collective-permute-start.2 = (f32[64,256]{1,0:T(8,128)S(1)}, f32[64,256]{1,0:T(8,128)S(1)}, u32[]{:S(2)}, u32[]{:S(2)}) collective-permute-start(f32[64,256]{1,0:T(8,128)S(1)} %get-tuple-element.16), channel_id=1, source_target_pairs={{0,1},{1,0},{2,3},{3,2},{4,5},{5,4},{6,7},{7,6},{8,9},{9,8},{10,11... | collective-permute-start | bytes 196616 | tf_op jit(solution)/shard_map/ppermute | solution.py:144
  17.5 1.4 %collective-permute-start.3 = (f32[64,256]{1,0:T(8,128)S(1)}, f32[64,256]{1,0:T(8,128)S(1)}, u32[]{:S(2)}, u32[]{:S(2)}) collective-permute-start(f32[64,256]{1,0:T(8,128)S(1)} %get-tuple-element.19), channel_id=1, source_target_pairs={{0,1},{1,0},{2,3},{3,2},{4,5},{5,4},{6,7},{7,6},{8,9},{9,8},{10,11... | collective-permute-start | bytes 196616 | tf_op jit(solution)/shard_map/ppermute | solution.py:144
  17.9 1.3 %collective-permute-start.4 = (f32[64,256]{1,0:T(8,128)S(1)}, f32[64,256]{1,0:T(8,128)S(1)}, u32[]{:S(2)}, u32[]{:S(2)}) collective-permute-start(f32[64,256]{1,0:T(8,128)S(1)} %get-tuple-element.18), channel_id=1, source_target_pairs={{0,1},{1,0},{2,3},{3,2},{4,5},{5,4},{6,7},{7,6},{8,9},{9,8},{10,11... | collective-permute-start | bytes 196616 | tf_op jit(solution)/shard_map/ppermute | solution.py:144
  18.0 1.3 %collective-permute-start.5 = (f32[64,256]{1,0:T(8,128)S(1)}, f32[64,256]{1,0:T(8,128)S(1)}, u32[]{:S(2)}, u32[]{:S(2)}) collective-permute-start(f32[64,256]{1,0:T(8,128)S(1)} %get-tuple-element.17), channel_id=1, source_target_pairs={{0,1},{1,0},{2,3},{3,2},{4,5},{5,4},{6,7},{7,6},{8,9},{9,8},{10,11... | collective-permute-start | bytes 196616 | tf_op jit(solution)/shard_map/ppermute | solution.py:144
  21.1 18.4 %collective-permute-start.6 = (f32[256,256]{1,0:T(8,128)S(1)}, f32[256,256]{1,0:T(8,128)S(1)}, u32[]{:S(2)}, u32[]{:S(2)}) collective-permute-start(f32[256,256]{1,0:T(8,128)S(1)} %middle.1), channel_id=1, source_target_pairs={{0,0},{32,1},{80,2},{240,3},{16,16},{48,17},{64,18},{224,19},{1,32... | collective-permute-start | bytes 786440 | tf_op jit(solution)/shard_map/ppermute | solution.py:165
  24.9 14.7 %collective-permute-start.7 = (f32[256,256]{1,0:T(8,128)S(1)}, f32[256,256]{1,0:T(8,128)}, u32[]{:S(2)}, u32[]{:S(2)}) collective-permute-start(f32[256,256]{1,0:T(8,128)S(1)} %middle.1), channel_id=1, source_target_pairs={{1,0},{33,1},{81,2},{241,3},{17,16},{49,17},{65,18},{225,19},{18,3... | collective-permute-start | bytes 786440 | tf_op jit(solution)/shard_map/ppermute | solution.py:165
  25.0 14.6 %collective-permute-start.8 = (f32[256,256]{1,0:T(8,128)S(1)}, f32[256,256]{1,0:T(8,128)}, u32[]{:S(2)}, u32[]{:S(2)}) collective-permute-start(f32[256,256]{1,0:T(8,128)S(1)} %middle.1), channel_id=1, source_target_pairs={{18,0},{50,1},{66,2},{226,3},{2,16},{34,17},{82,18},{242,19},{19,3... | collective-permute-start | bytes 786440 | tf_op jit(solution)/shard_map/ppermute | solution.py:165
  30.1 13.1 %collective-permute-start.9 = (f32[256,256]{1,0:T(8,128)S(1)}, f32[256,256]{1,0:T(8,128)}, u32[]{:S(2)}, u32[]{:S(2)}) collective-permute-start(f32[256,256]{1,0:T(8,128)S(1)} %middle.1), channel_id=1, source_target_pairs={{19,0},{51,1},{67,2},{227,3},{3,16},{35,17},{83,18},{243,19},{0,32... | collective-permute-start | bytes 786440 | tf_op jit(solution)/shard_map/ppermute | solution.py:165
  34.5 15.0 %all-to-all-start.1 = ((f32[8,8,512]{2,1,0:T(8,128)}), f32[8,8,512]{2,1,0:T(8,128)S(1)}, u32[]{:S(2)}, u32[]{:S(2)}) async-start(f32[8,8,512]{2,1,0:T(8,128)} %bitcast.6), calls=%async_computation.1 | async-start | bytes 262144 | tf_op jit(solution)/shard_map/all_to_all | solution.py:201
  39.5 17.8 %copy-start.2 = (f32[2,256,1024]{2,1,0:T(8,128)S(1)}, f32[2,256,1024]{2,1,0:T(8,128)}, u32[]{:S(2)}) copy-start(f32[2,256,1024]{2,1,0:T(8,128)} %inverse_hbm.1) | copy-start | bytes 6291460
  50.6 5.6 %collective-permute-start.10 = (f32[8,1280]{1,0:T(8,128)S(1)}, f32[8,1280]{1,0:T(8,128)S(1)}, u32[]{:S(2)}, u32[]{:S(2)}) collective-permute-start(f32[8,1280]{1,0:T(8,128)S(1)} %pad_maximum_fusion.5), channel_id=1, source_target_pairs={{0,3},{1,2},{2,1},{3,0},{4,7},{5,6},{6,5},{7,4},{8,11},{9,10},{10,... | collective-permute-start | bytes 122888 | tf_op jit(solution)/shard_map/ppermute | solution.py:152
  51.8 5.5 %collective-permute-start.11 = (f32[8,1280]{1,0:T(8,128)S(1)}, f32[8,1280]{1,0:T(8,128)S(1)}, u32[]{:S(2)}, u32[]{:S(2)}) collective-permute-start(f32[8,1280]{1,0:T(8,128)S(1)} %pad_maximum_fusion.5), channel_id=1, source_target_pairs={{0,2},{1,3},{2,0},{3,1},{4,6},{5,7},{6,4},{7,5},{8,10},{9,11},{10,... | collective-permute-start | bytes 122888 | tf_op jit(solution)/shard_map/ppermute | solution.py:152
  54.7 2.7 %collective-permute-start.12 = (f32[8,1280]{1,0:T(8,128)S(1)}, f32[8,1280]{1,0:T(8,128)S(1)}, u32[]{:S(2)}, u32[]{:S(2)}) collective-permute-start(f32[8,1280]{1,0:T(8,128)S(1)} %pad_maximum_fusion.5), channel_id=1, source_target_pairs={{0,1},{1,0},{2,3},{3,2},{4,5},{5,4},{6,7},{7,6},{8,9},{9,8},{10,11... | collective-permute-start | bytes 122888 | tf_op jit(solution)/shard_map/ppermute | solution.py:152
  60.4 4.4 %collective-permute-start.13 = (f32[8,1280]{1,0:T(8,128)S(1)}, f32[8,1280]{1,0:T(8,128)S(1)}, u32[]{:S(2)}, u32[]{:S(2)}) collective-permute-start(f32[8,1280]{1,0:T(8,128)S(1)} %get-tuple-element.25), channel_id=1, source_target_pairs={{0,1},{1,0},{2,3},{3,2},{4,5},{5,4},{6,7},{7,6},{8,9},{9,8},{10,11... | collective-permute-start | bytes 122888 | tf_op jit(solution)/shard_map/ppermute | solution.py:152
  61.0 4.4 %collective-permute-start.14 = (f32[8,1280]{1,0:T(8,128)S(1)}, f32[8,1280]{1,0:T(8,128)S(1)}, u32[]{:S(2)}, u32[]{:S(2)}) collective-permute-start(f32[8,1280]{1,0:T(8,128)S(1)} %get-tuple-element.26), channel_id=1, source_target_pairs={{0,2},{1,3},{2,0},{3,1},{4,6},{5,7},{6,4},{7,5},{8,10},{9,11},{10,... | collective-permute-start | bytes 122888 | tf_op jit(solution)/shard_map/ppermute | solution.py:152
  63.3 5.1 %collective-permute-start.15 = (f32[8,1280]{1,0:T(8,128)S(1)}, f32[8,1280]{1,0:T(8,128)S(1)}, u32[]{:S(2)}, u32[]{:S(2)}) collective-permute-start(f32[8,1280]{1,0:T(8,128)S(1)} %get-tuple-element.24), channel_id=1, source_target_pairs={{0,3},{1,2},{2,1},{3,0},{4,7},{5,6},{6,5},{7,4},{8,11},{9,10},{10,... | collective-permute-start | bytes 122888 | tf_op jit(solution)/shard_map/ppermute | solution.py:152

commit v4 on v3

--- a/solution.py
+++ b/solution.py
@@ -148,8 +148,12 @@
     return lax.ppermute(block, NEAR, [(s, s ^ 6) for s in range(8)])
 
 
-def from_col(block, flip):
-    return lax.ppermute(block, COL, [(s, s ^ flip) for s in range(4)])
+def opposite(block):
+    return lax.ppermute(block, "xh", [(0, 1), (1, 0)])
+
+
+def ordered(second, here, there):
+    return jnp.concatenate([jnp.where(second == 1, there, here), jnp.where(second == 1, here, there)], axis=1)
 
 
 def from_quad(block, turn):
@@ -180,10 +184,6 @@
     return lax.dynamic_slice_in_dim(array, index * 256, 256, 1)
 
 
-def added(blocks):
-    return (blocks[0] + blocks[1]) + (blocks[2] + blocks[3])
-
-
 def shards(factor_rows, solved_rows, right_side, inverse, coupling):
     mine = lax.axis_index(COL)
     quad = lax.axis_index("z") % 4
@@ -199,24 +199,29 @@
     part = after(sum_parts(part), middle)
     columns = [from_quad(middle, k) for k in range(4)]
     part = lax.all_to_all(part.reshape(8, 8, 512), "z", 0, 0, tiled=True)
-    r = after(part.sum(0), columns)
+    r = part.sum(0)
     columns = turned(columns, quad)
     rows = jnp.concatenate([c.T for c in columns], axis=1)
     columns = jnp.concatenate(columns, axis=0)
 
     r0, r1 = r[:, :256], r[:, 256:]
     s = jnp.concatenate([jnp.where(mine == k, r1, 0.0) for k in range(4)], axis=1) - exact(r0, rows, ((1,), (0,)))
+    core, xh = lax.axis_index("core"), lax.axis_index("xh")
     sent = jnp.concatenate([r0, s], axis=1)
-    got = [sent] + [from_col(sent, k) for k in (1, 2, 3)]
-    f0 = exact(jnp.concatenate(in_order([g[:, :256] for g in got], mine), axis=1), inverse[0], ((1,), (1,)))
-    f1 = exact(added([g[:, 256:] for g in got]), inverse[1], ((1,), (1,)))
+    other = near(sent)
+    pair = ordered(core, sent[:, :256], other[:, :256])
+    sent = jnp.concatenate([pair, sent[:, 256:] + other[:, 256:]], axis=1)
+    other = opposite(sent)
+    f0 = exact(ordered(xh, sent[:, :512], other[:, :512]), inverse[0], ((1,), (1,)))
+    f1 = exact(sent[:, 512:] + other[:, 512:], inverse[1], ((1,), (1,)))
     b0 = exact(f0, inverse[0], ((1,), (0,)))
     b1 = exact(f1, inverse[1], ((1,), (0,)))
-    sent = [jnp.concatenate([block_of(b0, mine ^ k), b1], axis=1) for k in range(4)]
-    got = [sent[0]] + [from_col(sent[k], k) for k in (1, 2, 3)]
-    b = added(got)
-    b1 = b[:, 256:]
-    b0 = b[:, :256] - exact(b1, columns, ((1,), (0,)))
+    other = near(jnp.concatenate([b1, block_of(b0, mine ^ 1), block_of(b0, mine ^ 3)], axis=1))
+    sums = jnp.concatenate([b1, block_of(b0, mine), block_of(b0, mine ^ 2)], axis=1) + other
+    other = opposite(jnp.concatenate([sums[:, :1024], sums[:, 1280:]], axis=1))
+    b = sums[:, :1280] + other
+    b1 = b[:, :1024]
+    b0 = b[:, 1024:] - exact(b1, columns, ((1,), (0,)))
     forward = jnp.stack([f0, f1])
     backward = jnp.stack([b0, block_of(b1, mine)])
     return (forward.transpose(0, 2, 1), backward.transpose(0, 2, 1))

time: 69.9 us -> 68.2 us (0.976)
  waiting for transfers between devices: 16 us -> 14.9 us
  starting transfers between devices: 35.6 us -> 34.9 us
    ppermute x6 -> x2, starting transfers between devices: 7.86 us -> 2.96 us  [opposite(): return lax.ppermute(block, 'xh', [(0, 1), (1, 0)])]
    ppermute x5 -> x7, starting transfers between devices: 2.34 us -> 6.4 us  [near(): return lax.ppermute(block, 'core', [(0, 1), (1, 0)])]
    ppermute x5 -> x7, waiting for transfers between devices: 0.9 us -> 2.65 us  [near(): return lax.ppermute(block, 'core', [(0, 1), (1, 0)])]
    ppermute x4, waiting for transfers between devices: 3.58 us -> 2.11 us  [from_quad(): return lax.ppermute(block, ('z', 'xl', 'xh', 'core'), pairs)]
    ppermute x6 -> x2, waiting for transfers between devices: 6.31 us -> 5.41 us  [opposite(): return lax.ppermute(block, 'xh', [(0, 1), (1, 0)])]
    all_to_all x1, starting transfers between devices: 5 us -> 5.88 us  [shards(): part = lax.all_to_all(part.reshape(8, 8, 512), 'z', 0, 0, tiled=True)]
    ppermute x4, starting transfers between devices: 12.7 us -> 11.9 us  [from_quad(): return lax.ppermute(block, ('z', 'xl', 'xh', 'core'), pairs)]
  transfers between devices with their start and end apart: 18 -> 16, of which waited for: 10 -> 10; matrix products, arithmetic and copies ran while one was open for 3% -> 3% of each run, Pallas kernels for 6% -> 6%
where the time goes in v4:
time: 68.2 us; the launch traced here: 67.8 us
  starting transfers between devices  34.9 us (51%)
  waiting for transfers between devices  14.9 us (22%)
  Pallas kernels  10 us (15%)
  matrix products  4.56 us (7%)
  other arithmetic  2.59 us (4%)
  between operations  0.87 us (1%)
    ppermute x4, starting transfers between devices, from_quad(): return lax.ppermute(block, ('z', 'xl', 'xh', 'core'), pairs)  11.9 us
    ppermute x7, starting transfers between devices, near(): return lax.ppermute(block, 'core', [(0, 1), (1, 0)])  6.4 us
    all_to_all x1, starting transfers between devices, shards(): part = lax.all_to_all(part.reshape(8, 8, 512), 'z', 0, 0, tiled=True)  5.88 us
    pallas_call x1, Pallas kernels, product(): pl.pallas_call(product_kernel, in_specs=[pl.BlockSpec(memory_space=pltpu....  5.72 us
    ppermute x2, waiting for transfers between devices, opposite(): return lax.ppermute(block, 'xh', [(0, 1), (1, 0)])  5.41 us
    all_to_all x1, waiting for transfers between devices, shards(): part = lax.all_to_all(part.reshape(8, 8, 512), 'z', 0, 0, tiled=True)  4.69 us
    dot_general x6, matrix products, exact(): lax.dot_general(left, right, (dims, ((), ())), preferred_element_type=jnp...  4.56 us
    all_to_all x1, starting transfers between devices, shards(): part = lax.all_to_all(part, ('xl', 'y'), 0, 0, tiled=True)  4.33 us
  transfers between devices with their start and end apart: 16, of which 10 were waited for; matrix products, arithmetic and copies ran while one was open for 3% of the time, Pallas kernels for 6%

profile of v4, /device:TPU:1, one launch (start us, length us, event | category | flops | bytes accessed | tf_op | source)
XLA Modules:
  0.0 67.8 jit_solution(14096607645893222535)
XLA Ops:
  0.7 0.1 pad_add_fusion.at_ref
  0.7 5.7 %product.1 = (f32[512,512]{1,0:T(8,128)S(1)}, f32[256,256]{1,0:T(8,128)S(1)}) custom-call(s32[4]{0:T(128)S(1)} %pad_add_fusion.at_ref, f32[512,2048]{1,0:T(8,128)} %bitcast.40, f32[2048,512]{1,0:T(8,128)} %solved_hbm.1, f32[2,256,1024]{2,1,0:T(8,128)} %inverse_hbm.1), custom_call_target="tpu_custom_call" | custom-call | flops 3221225472 | bytes 9437184 | tf_op jit(solution)/shard_map/product/pallas_call | solution.py:53
  6.5 3.4 %collective-permute-start.1 = (f32[256,256]{1,0:T(8,128)S(1)}, f32[256,256]{1,0:T(8,128)S(1)}, u32[]{:S(2)}, u32[]{:S(2)}) collective-permute-start(f32[256,256]{1,0:T(8,128)S(1)} %get-tuple-element.7.p0), channel_id=1, source_target_pairs={{0,18},{1,19},{2,16},{3,17},{16,2},{17,3},{18,0},{19,1},{4,22},{5,... | collective-permute-start | bytes 786440 | tf_op jit(solution)/shard_map/ppermute | solution.py:148
  9.9 0.0 copy-done.1
  9.9 1.9 %place.1 = f32[8,64,512]{2,1,0:T(8,128)} custom-call(s32[4]{0:T(128)S(1)} %pad_add_fusion.at_ref, f32[512,512]{1,0:T(8,128)S(1)} %get-tuple-element.6.update_ref, f32[2,8,256]{2,1,0:T(8,128)S(1)} %bitcast.33), custom_call_target="tpu_custom_call" | custom-call | flops 262144 | bytes 2097152 | tf_op jit(solution)/shard_map/place/pallas_call | solution.py:82
  11.8 4.3 %all-to-all-start = ((f32[8,64,512]{2,1,0:T(8,128)}), f32[8,64,512]{2,1,0:T(8,128)S(1)}, u32[]{:S(2)}, u32[]{:S(2)}) async-start(f32[8,64,512]{2,1,0:T(8,128)} %place.1), calls=%async_computation | async-start | bytes 2097152 | tf_op jit(solution)/shard_map/all_to_all | solution.py:196
  16.1 1.2 %collective-permute-start = (f32[256,256]{1,0:T(8,128)S(1)}, f32[256,256]{1,0:T(8,128)S(1)}, u32[]{:S(2)}, u32[]{:S(2)}) collective-permute-start(f32[256,256]{1,0:T(8,128)S(1)} %get-tuple-element.7.p0), channel_id=1, source_target_pairs={{0,1},{1,0},{2,3},{3,2},{4,5},{5,4},{6,7},{7,6},{8,9},{9,8},{10,11... | collective-permute-start | bytes 786440 | tf_op jit(solution)/shard_map/ppermute | solution.py:144
  17.3 0.0 collective-permute-done.1.p2
  17.3 0.1 collective-permute-start.2
  17.5 0.4 collective-permute-start.3
  17.9 0.1 collective-permute-start.4
  18.0 0.4 collective-permute-start.5
  18.4 0.2 collective-permute-done.2
  18.7 0.2 collective-permute-done.3
  18.8 0.4 collective-permute-done.4
  19.2 0.2 collective-permute-done.5
  19.4 0.0 collective-permute-done.p1
  19.4 0.0 copy-done
  19.4 1.7 %middle.1 = f32[256,256]{1,0:T(8,128)S(1)} custom-call(s32[4]{0:T(128)S(1)} %pad_add_fusion.at_ref, f32[256,1024]{1,0:T(8,128)S(1)} %copy-done, f32[256,256]{1,0:T(8,128)S(1)} %get-tuple-element.7.p0, f32[256,256]{1,0:T(8,128)S(1)} %collective-permute-done.p1, f32[256,256]{1,0:T(8,128)S(1)} %collective-permute-done.1.p2, f32[256,256]{1,0:T(8,128)S(1)} %pad_maximum_fusion.p3), custom_call_target="tpu_custom_call" | custom-call | flops 1024 | bytes 1024 | tf_op jit(solution)/shard_map/middle/pallas_call | solution.py:131
  21.1 0.4 collective-permute-start.6
  21.6 7.8 %collective-permute-start.7 = (f32[256,256]{1,0:T(8,128)S(1)}, f32[256,256]{1,0:T(8,128)}, u32[]{:S(2)}, u32[]{:S(2)}) collective-permute-start(f32[256,256]{1,0:T(8,128)S(1)} %middle.1), channel_id=1, source_target_pairs={{18,0},{50,1},{66,2},{226,3},{2,16},{34,17},{82,18},{242,19},{19,3... | collective-permute-start | bytes 786440 | tf_op jit(solution)/shard_map/ppermute | solution.py:169
  29.4 1.5 %collective-permute-start.8 = (f32[256,256]{1,0:T(8,128)S(1)}, f32[256,256]{1,0:T(8,128)}, u32[]{:S(2)}, u32[]{:S(2)}) collective-permute-start(f32[256,256]{1,0:T(8,128)S(1)} %middle.1), channel_id=1, source_target_pairs={{19,0},{51,1},{67,2},{227,3},{3,16},{35,17},{83,18},{243,19},{0,32... | collective-permute-start | bytes 786440 | tf_op jit(solution)/shard_map/ppermute | solution.py:169
  30.9 2.1 %collective-permute-start.9 = (f32[256,256]{1,0:T(8,128)S(1)}, f32[256,256]{1,0:T(8,128)}, u32[]{:S(2)}, u32[]{:S(2)}) collective-permute-start(f32[256,256]{1,0:T(8,128)S(1)} %middle.1), channel_id=1, source_target_pairs={{0,0},{32,1},{80,2},{240,3},{16,16},{48,17},{64,18},{224,19},{1,32... | collective-permute-start | bytes 786440 | tf_op jit(solution)/shard_map/ppermute | solution.py:169
  33.1 0.0 all-to-all-done.parts_ref
  33.1 0.7 %sum_parts.1 = f32[64,512]{1,0:T(8,128)} custom-call(f32[8,64,512]{2,1,0:T(8,128)S(1)} %all-to-all-done.parts_ref), custom_call_target="tpu_custom_call" | custom-call | flops 262144 | bytes 1048576 | tf_op jit(solution)/shard_map/sum_parts/pallas_call | solution.py:102
  33.8 5.9 %all-to-all-start.1 = ((f32[8,8,512]{2,1,0:T(8,128)}), f32[8,8,512]{2,1,0:T(8,128)S(1)}, u32[]{:S(2)}, u32[]{:S(2)}) async-start(f32[8,8,512]{2,1,0:T(8,128)} %bitcast.6), calls=%async_computation.1 | async-start | bytes 262144 | tf_op jit(solution)/shard_map/all_to_all | solution.py:201
  39.6 0.0 collective-permute-done.6
  39.7 0.0 collective-permute-done.7
  39.7 2.1 %collective-permute-done.8 = f32[256,256]{1,0:T(8,128)} collective-permute-done((f32[256,256]{1,0:T(8,128)S(1)}, f32[256,256]{1,0:T(8,128)}, u32[]{:S(2)}, u32[]{:S(2)}) %collective-permute-start.8) | collective-permute-done | bytes 262176 | tf_op jit(solution)/shard_map/ppermute | solution.py:169
  41.8 0.0 collective-permute-done.9
  41.8 1.2 %broadcast_select_fusion.7 = (f32[256,256]{1,0:T(8,128)S(1)}, f32[256,256]{1,0:T(8,128)S(1)}, f32[256,256]{1,0:T(8,128)S(1)}, f32[256,256]{1,0:T(8,128)S(1)}) fusion(pred[]{:T(512)S(6)} %eq.44, f32[256,256]{1,0:T(8,128)S(1)} %collective-permute-done.6, f32[256,256]{1,0:T(8,128)} %collective-permute-done.7, pred[]{:T(512)S(6)} %eq.45, ...), kind=kLoop, calls=%fused_computation.36 | loop fusion | flops 524288 | bytes 2097154 | tf_op jit(solution)/shard_map/jit(_where)/select_n | solution.py:180
  43.0 4.7 %all-to-all-done.1 = f32[8,8,512]{2,1,0:T(8,128)S(1)} async-done(((f32[8,8,512]{2,1,0:T(8,128)}), f32[8,8,512]{2,1,0:T(8,128)S(1)}, u32[]{:S(2)}, u32[]{:S(2)}) %all-to-all-start.1) | async-done | bytes 131104 | tf_op jit(solution)/shard_map/all_to_all | solution.py:201
  47.7 1.0 %convolution_subtract_fusion = f32[8,1024]{1,0:T(8,128)S(1)} fusion(f32[256,256]{0,1:T(8,128)S(1)} %bitcast.37, f32[256,256]{0,1:T(8,128)S(1)} %bitcast.36, f32[256,256]{0,1:T(8,128)S(1)} %bitcast.35, f32[256,256]{0,1:T(8,128)S(1)} %bitcast.34, f32[8,256]{1,0:T(8,128)S(1)} %get-tuple-element.29, f32[8,256]{1,0:T(8,128)S(1)} %get-tuple-element.28, ...), kind=kOutput, calls=%fused_computation | convolution fusion | flops 25985024 | bytes 1122304 | tf_op jit(solution)/shard_map/dot_general | solution.py:118
  48.7 2.5 %collective-permute-start.10 = (f32[8,1280]{1,0:T(8,128)S(1)}, f32[8,1280]{1,0:T(8,128)S(1)}, u32[]{:S(2)}, u32[]{:S(2)}) collective-permute-start(f32[8,1280]{1,0:T(8,128)S(1)} %pad_maximum_fusion.4), channel_id=1, source_target_pairs={{0,1},{1,0},{2,3},{3,2},{4,5},{5,4},{6,7},{7,6},{8,9},{9,8},{10,11... | collective-permute-start | bytes 122888 | tf_op jit(solution)/shard_map/ppermute | solution.py:144
  51.1 0.9 %collective-permute-done.10 = f32[8,1280]{1,0:T(8,128)S(1)} collective-permute-done((f32[8,1280]{1,0:T(8,128)S(1)}, f32[8,1280]{1,0:T(8,128)S(1)}, u32[]{:S(2)}, u32[]{:S(2)}) %collective-permute-start.10) | collective-permute-done | bytes 40992 | tf_op jit(solution)/shard_map/ppermute | solution.py:144
  52.0 1.5 %collective-permute-start.11 = (f32[8,1536]{1,0:T(8,128)S(1)}, f32[8,1536]{1,0:T(8,128)S(1)}, u32[]{:S(2)}, u32[]{:S(2)}) collective-permute-start(f32[8,1536]{1,0:T(8,128)S(1)} %pad_maximum_fusion.3), channel_id=1, source_target_pairs={{0,2},{2,0},{1,3},{3,1},{4,6},{6,4},{5,7},{7,5},{8,10},{10,8},{9,1... | collective-permute-start | bytes 147464 | tf_op jit(solution)/shard_map/ppermute | solution.py:152
  53.5 3.1 %collective-permute-done.11 = f32[8,1536]{1,0:T(8,128)S(1)} collective-permute-done((f32[8,1536]{1,0:T(8,128)S(1)}, f32[8,1536]{1,0:T(8,128)S(1)}, u32[]{:S(2)}, u32[]{:S(2)}) %collective-permute-start.11) | collective-permute-done | bytes 49184 | tf_op jit(solution)/shard_map/ppermute | solution.py:152
  56.6 0.9 %fusion.21 = f32[8,256]{1,0:T(8,128)S(1)} fusion(f32[2,256,1024]{2,1,0:T(8,128)S(1)} %copy-done.2, f32[8,512]{1,0:T(8,128)S(1)} %get-tuple-element.19, f32[8,512]{1,0:T(8,128)S(1)} %get-tuple-element.18), kind=kOutput, calls=%fused_computation.22 | convolution fusion | flops 25174016 | bytes 1089536 | tf_op jit(solution)/shard_map/dot_general | solution.py:118
  57.5 0.6 fusion.19
  58.1 0.9 %fusion.17 = f32[8,256]{1,0:T(8,128)S(1)} fusion(f32[2,256,1024]{2,1,0:T(8,128)S(1)} %copy-done.2, f32[8,1024]{1,0:T(8,128)S(1)} %slice_add_fusion.3, f32[8,1536]{1,0:T(8,128)S(1)} %collective-permute-done.11), kind=kOutput, calls=%fused_computation.18 | convolution fusion | flops 25174016 | bytes 1122304 | tf_op jit(solution)/shard_map/dot_general | solution.py:118
  59.0 0.6 fusion.15
  59.7 1.6 %collective-permute-start.12 = (f32[8,1536]{1,0:T(8,128)S(1)}, f32[8,1536]{1,0:T(8,128)S(1)}, u32[]{:S(2)}, u32[]{:S(2)}) collective-permute-start(f32[8,1536]{1,0:T(8,128)S(1)} %fusion.29), channel_id=1, source_target_pairs={{0,1},{1,0},{2,3},{3,2},{4,5},{5,4},{6,7},{7,6},{8,9},{9,8},{10,11... | collective-permute-start | bytes 147464 | tf_op jit(solution)/shard_map/ppermute | solution.py:144
  61.3 0.9 %collective-permute-done.12 = f32[8,1536]{1,0:T(8,128)S(1)} collective-permute-done((f32[8,1536]{1,0:T(8,128)S(1)}, f32[8,1536]{1,0:T(8,128)S(1)}, u32[]{:S(2)}, u32[]{:S(2)}) %collective-permute-start.12) | collective-permute-done | bytes 49184 | tf_op jit(solution)/shard_map/ppermute | solution.py:144
  62.2 1.5 %collective-permute-start.13 = (f32[8,1280]{1,0:T(8,128)S(1)}, f32[8,1280]{1,0:T(8,128)S(1)}, u32[]{:S(2)}, u32[]{:S(2)}) collective-permute-start(f32[8,1280]{1,0:T(8,128)S(1)} %pad_maximum_fusion.5), channel_id=1, source_target_pairs={{0,2},{2,0},{1,3},{3,1},{4,6},{6,4},{5,7},{7,5},{8,10},{10,8},{9,1... | collective-permute-start | bytes 122888 | tf_op jit(solution)/shard_map/ppermute | solution.py:152
  63.7 0.6 maximum_bitcast_fusion
  64.3 2.4 %collective-permute-done.13 = f32[8,1280]{1,0:T(8,128)S(1)} collective-permute-done((f32[8,1280]{1,0:T(8,128)S(1)}, f32[8,1280]{1,0:T(8,128)S(1)}, u32[]{:S(2)}, u32[]{:S(2)}) %collective-permute-start.13) | collective-permute-done | bytes 40992 | tf_op jit(solution)/shard_map/ppermute | solution.py:152
  66.6 0.5 fusion.33
  67.2 0.6 maximum_bitcast_fusion.1
  (22 shorter events, 0.1 us)
Async XLA Ops:
  0.7 9.1 %copy-start.1 = (f32[2,256,8]{1,2,0:T(8,128)S(1)}, f32[2,256,8]{1,2,0:T(8,128)}, u32[]{:S(2)}) copy-start(f32[2,256,8]{1,2,0:T(8,128)} %param.7) | copy-start | bytes 49156
  6.5 10.9 %collective-permute-start.1 = (f32[256,256]{1,0:T(8,128)S(1)}, f32[256,256]{1,0:T(8,128)S(1)}, u32[]{:S(2)}, u32[]{:S(2)}) collective-permute-start(f32[256,256]{1,0:T(8,128)S(1)} %get-tuple-element.7.p0), channel_id=1, source_target_pairs={{0,18},{1,19},{2,16},{3,17},{16,2},{17,3},{18,0},{19,1},{4,22},{5,... | collective-permute-start | bytes 786440 | tf_op jit(solution)/shard_map/ppermute | solution.py:148
  11.7 7.6 %copy-start = (f32[256,1024]{1,0:T(8,128)S(1)}, f32[256,1024]{1,0:T(8,128)}, u32[]{:S(2)}) copy-start(f32[256,1024]{1,0:T(8,128)} %left_ref.1) | copy-start | bytes 3145732
  11.8 21.3 %all-to-all-start = ((f32[8,64,512]{2,1,0:T(8,128)}), f32[8,64,512]{2,1,0:T(8,128)S(1)}, u32[]{:S(2)}, u32[]{:S(2)}) async-start(f32[8,64,512]{2,1,0:T(8,128)} %place.1), calls=%async_computation | async-start | bytes 2097152 | tf_op jit(solution)/shard_map/all_to_all | solution.py:196
  16.1 3.3 %collective-permute-start = (f32[256,256]{1,0:T(8,128)S(1)}, f32[256,256]{1,0:T(8,128)S(1)}, u32[]{:S(2)}, u32[]{:S(2)}) collective-permute-start(f32[256,256]{1,0:T(8,128)S(1)} %get-tuple-element.7.p0), channel_id=1, source_target_pairs={{0,1},{1,0},{2,3},{3,2},{4,5},{5,4},{6,7},{7,6},{8,9},{9,8},{10,11... | collective-permute-start | bytes 786440 | tf_op jit(solution)/shard_map/ppermute | solution.py:144
  17.3 1.3 %collective-permute-start.2 = (f32[64,256]{1,0:T(8,128)S(1)}, f32[64,256]{1,0:T(8,128)S(1)}, u32[]{:S(2)}, u32[]{:S(2)}) collective-permute-start(f32[64,256]{1,0:T(8,128)S(1)} %get-tuple-element.14), channel_id=1, source_target_pairs={{0,1},{1,0},{2,3},{3,2},{4,5},{5,4},{6,7},{7,6},{8,9},{9,8},{10,11... | collective-permute-start | bytes 196616 | tf_op jit(solution)/shard_map/ppermute | solution.py:144
  17.5 1.4 %collective-permute-start.3 = (f32[64,256]{1,0:T(8,128)S(1)}, f32[64,256]{1,0:T(8,128)S(1)}, u32[]{:S(2)}, u32[]{:S(2)}) collective-permute-start(f32[64,256]{1,0:T(8,128)S(1)} %get-tuple-element.17), channel_id=1, source_target_pairs={{0,1},{1,0},{2,3},{3,2},{4,5},{5,4},{6,7},{7,6},{8,9},{9,8},{10,11... | collective-permute-start | bytes 196616 | tf_op jit(solution)/shard_map/ppermute | solution.py:144
  17.9 1.3 %collective-permute-start.4 = (f32[64,256]{1,0:T(8,128)S(1)}, f32[64,256]{1,0:T(8,128)S(1)}, u32[]{:S(2)}, u32[]{:S(2)}) collective-permute-start(f32[64,256]{1,0:T(8,128)S(1)} %get-tuple-element.16), channel_id=1, source_target_pairs={{0,1},{1,0},{2,3},{3,2},{4,5},{5,4},{6,7},{7,6},{8,9},{9,8},{10,11... | collective-permute-start | bytes 196616 | tf_op jit(solution)/shard_map/ppermute | solution.py:144
  18.0 1.3 %collective-permute-start.5 = (f32[64,256]{1,0:T(8,128)S(1)}, f32[64,256]{1,0:T(8,128)S(1)}, u32[]{:S(2)}, u32[]{:S(2)}) collective-permute-start(f32[64,256]{1,0:T(8,128)S(1)} %get-tuple-element.15), channel_id=1, source_target_pairs={{0,1},{1,0},{2,3},{3,2},{4,5},{5,4},{6,7},{7,6},{8,9},{9,8},{10,11... | collective-permute-start | bytes 196616 | tf_op jit(solution)/shard_map/ppermute | solution.py:144
  21.1 18.5 %collective-permute-start.6 = (f32[256,256]{1,0:T(8,128)S(1)}, f32[256,256]{1,0:T(8,128)S(1)}, u32[]{:S(2)}, u32[]{:S(2)}) collective-permute-start(f32[256,256]{1,0:T(8,128)S(1)} %middle.1), channel_id=1, source_target_pairs={{1,0},{33,1},{81,2},{241,3},{17,16},{49,17},{65,18},{225,19},{18,3... | collective-permute-start | bytes 786440 | tf_op jit(solution)/shard_map/ppermute | solution.py:169
  21.6 18.1 %collective-permute-start.7 = (f32[256,256]{1,0:T(8,128)S(1)}, f32[256,256]{1,0:T(8,128)}, u32[]{:S(2)}, u32[]{:S(2)}) collective-permute-start(f32[256,256]{1,0:T(8,128)S(1)} %middle.1), channel_id=1, source_target_pairs={{18,0},{50,1},{66,2},{226,3},{2,16},{34,17},{82,18},{242,19},{19,3... | collective-permute-start | bytes 786440 | tf_op jit(solution)/shard_map/ppermute | solution.py:169
  29.4 12.4 %collective-permute-start.8 = (f32[256,256]{1,0:T(8,128)S(1)}, f32[256,256]{1,0:T(8,128)}, u32[]{:S(2)}, u32[]{:S(2)}) collective-permute-start(f32[256,256]{1,0:T(8,128)S(1)} %middle.1), channel_id=1, source_target_pairs={{19,0},{51,1},{67,2},{227,3},{3,16},{35,17},{83,18},{243,19},{0,32... | collective-permute-start | bytes 786440 | tf_op jit(solution)/shard_map/ppermute | solution.py:169
  30.9 10.9 %collective-permute-start.9 = (f32[256,256]{1,0:T(8,128)S(1)}, f32[256,256]{1,0:T(8,128)}, u32[]{:S(2)}, u32[]{:S(2)}) collective-permute-start(f32[256,256]{1,0:T(8,128)S(1)} %middle.1), channel_id=1, source_target_pairs={{0,0},{32,1},{80,2},{240,3},{16,16},{48,17},{64,18},{224,19},{1,32... | collective-permute-start | bytes 786440 | tf_op jit(solution)/shard_map/ppermute | solution.py:169
  33.8 13.9 %all-to-all-start.1 = ((f32[8,8,512]{2,1,0:T(8,128)}), f32[8,8,512]{2,1,0:T(8,128)S(1)}, u32[]{:S(2)}, u32[]{:S(2)}) async-start(f32[8,8,512]{2,1,0:T(8,128)} %bitcast.6), calls=%async_computation.1 | async-start | bytes 262144 | tf_op jit(solution)/shard_map/all_to_all | solution.py:201
  39.6 16.9 %copy-start.2 = (f32[2,256,1024]{2,1,0:T(8,128)S(1)}, f32[2,256,1024]{2,1,0:T(8,128)}, u32[]{:S(2)}) copy-start(f32[2,256,1024]{2,1,0:T(8,128)} %inverse_hbm.1) | copy-start | bytes 6291460
  48.7 3.3 %collective-permute-start.10 = (f32[8,1280]{1,0:T(8,128)S(1)}, f32[8,1280]{1,0:T(8,128)S(1)}, u32[]{:S(2)}, u32[]{:S(2)}) collective-permute-start(f32[8,1280]{1,0:T(8,128)S(1)} %pad_maximum_fusion.4), channel_id=1, source_target_pairs={{0,1},{1,0},{2,3},{3,2},{4,5},{5,4},{6,7},{7,6},{8,9},{9,8},{10,11... | collective-permute-start | bytes 122888 | tf_op jit(solution)/shard_map/ppermute | solution.py:144
  52.0 4.5 %collective-permute-start.11 = (f32[8,1536]{1,0:T(8,128)S(1)}, f32[8,1536]{1,0:T(8,128)S(1)}, u32[]{:S(2)}, u32[]{:S(2)}) collective-permute-start(f32[8,1536]{1,0:T(8,128)S(1)} %pad_maximum_fusion.3), channel_id=1, source_target_pairs={{0,2},{2,0},{1,3},{3,1},{4,6},{6,4},{5,7},{7,5},{8,10},{10,8},{9,1... | collective-permute-start | bytes 147464 | tf_op jit(solution)/shard_map/ppermute | solution.py:152
  59.7 2.5 %collective-permute-start.12 = (f32[8,1536]{1,0:T(8,128)S(1)}, f32[8,1536]{1,0:T(8,128)S(1)}, u32[]{:S(2)}, u32[]{:S(2)}) collective-permute-start(f32[8,1536]{1,0:T(8,128)S(1)} %fusion.29), channel_id=1, source_target_pairs={{0,1},{1,0},{2,3},{3,2},{4,5},{5,4},{6,7},{7,6},{8,9},{9,8},{10,11... | collective-permute-start | bytes 147464 | tf_op jit(solution)/shard_map/ppermute | solution.py:144
  62.2 4.4 %collective-permute-start.13 = (f32[8,1280]{1,0:T(8,128)S(1)}, f32[8,1280]{1,0:T(8,128)S(1)}, u32[]{:S(2)}, u32[]{:S(2)}) collective-permute-start(f32[8,1280]{1,0:T(8,128)S(1)} %pad_maximum_fusion.5), channel_id=1, source_target_pairs={{0,2},{2,0},{1,3},{3,1},{4,6},{6,4},{5,7},{7,5},{8,10},{10,8},{9,1... | collective-permute-start | bytes 122888 | tf_op jit(solution)/shard_map/ppermute | solution.py:152

commit v5 on v4

--- a/solution.py
+++ b/solution.py
@@ -31,17 +31,18 @@
         pair[0].start()
         pair[1].start()
         copies.append(pair)
-    for k in range(STEPS):
-        copies[k][0].wait()
-        copies[k][1].wait()
-        fh, fl = split(factor_ref[:, k * DEPTH : (k + 1) * DEPTH])
-        sh, sl = split(solved_ref[k * DEPTH : (k + 1) * DEPTH, :])
+    for first, count in ((0, 2), (2, 2), (4, 2), (6, 1), (7, 1)):
+        for k in range(first, first + count):
+            copies[k][0].wait()
+            copies[k][1].wait()
+        fh, fl = split(factor_ref[:, first * DEPTH : (first + count) * DEPTH])
+        sh, sl = split(solved_ref[first * DEPTH : (first + count) * DEPTH, :])
         term = jnp.dot(
             jnp.concatenate([fh, fh, fl], axis=1),
             jnp.concatenate([sh, sl, sh], axis=0),
             preferred_element_type=jnp.float32,
         )
-        if k == 0:
+        if first == 0:
             slab.start()
             out_ref[...] = term
         else:
@@ -67,14 +68,26 @@
     )(at, *(pltpu.with_memory_space_constraint(x, pltpu.HBM) for x in (flat, solved_rows, inverse)))
 
 
-def place_kernel(at_ref, update_ref, right_ref, out_ref):
-    turned = -update_ref[...].T
-    for z in range(8):
-        for p in range(8):
-            out_ref[p, pl.ds(8 * z, 8), :] = turned[64 * z + 8 * p : 64 * z + 8 * p + 8, :]
-    rows = pl.ds(pl.multiple_of(at_ref[1] * 8, 8), 8)
-    out_ref[at_ref[0], rows, 0:256] += right_ref[0]
-    out_ref[at_ref[0], rows, 256:512] += right_ref[1]
+def place_kernel(at_ref, update_ref, right_ref, out_hbm, out_ref, sem):
+    copies = []
+    for part in range(4):
+        turned = -update_ref[:, 128 * part : 128 * part + 128].T
+        for half in range(2):
+            rows = slice(16 * part + 8 * half, 16 * part + 8 * half + 8)
+            for p in range(8):
+                out_ref[p, rows, :] = turned[64 * half + 8 * p : 64 * half + 8 * p + 8, :]
+
+        @pl.when(at_ref[1] // 2 == part)
+        def _():
+            rows = pl.ds(pl.multiple_of(at_ref[1] * 8, 8), 8)
+            out_ref[at_ref[0], rows, 0:256] += right_ref[0]
+            out_ref[at_ref[0], rows, 256:512] += right_ref[1]
+
+        rows = pl.ds(16 * part, 16)
+        copies.append(pltpu.make_async_copy(out_ref.at[:, rows, :], out_hbm.at[:, rows, :], sem.at[part]))
+        copies[-1].start()
+    for copy in copies:
+        copy.wait()
 
 
 def place(at, update, right):
@@ -82,8 +95,9 @@
     return pl.pallas_call(
         place_kernel,
         in_specs=[pl.BlockSpec(memory_space=pltpu.SMEM), vmem, vmem],
-        out_specs=vmem,
+        out_specs=pl.BlockSpec(memory_space=pl.ANY),
         out_shape=jax.ShapeDtypeStruct((8, 64, 512), jnp.float32),
+        scratch_shapes=[pltpu.VMEM((8, 64, 512), jnp.float32), pltpu.SemaphoreType.DMA((4,))],
         compiler_params=pltpu.CompilerParams(vmem_limit_bytes=8 << 20),
         cost_estimate=pl.CostEstimate(flops=1 << 18, bytes_accessed=2 << 20, transcendentals=0),
         name="place",
@@ -116,7 +130,7 @@
 
 def exact(left, right, dims):
     return lax.dot_general(
-        left, right, (dims, ((), ())), preferred_element_type=jnp.float32, precision=lax.Precision.HIGHEST
+        left, right, (dims, ((), ())), preferred_element_type=jnp.float32, precision=lax.Precision.HIGH
     )
 
 
@@ -126,7 +140,13 @@
     def kernel(at_ref, left_ref, p0, p1, p2, p3, out_ref, whole_ref):
         for flip, piece in enumerate((p0, p1, p2, p3)):
             whole_ref[pl.ds(pl.multiple_of((at_ref[3] ^ flip) * 256, 256), 256), :] = piece[...]
-        out_ref[...] = exact(left_ref[...], whole_ref[...], ((1,), (0,)))
+        ah, al = split(left_ref[...])
+        bh, bl = split(whole_ref[...])
+        out_ref[...] = jnp.dot(
+            jnp.concatenate([ah, ah, al], axis=1),
+            jnp.concatenate([bh, bl, bh], axis=0),
+            preferred_element_type=jnp.float32,
+        )
 
     return pl.pallas_call(
         kernel,

time: 68.2 us -> 66.5 us (0.975)
  matrix products: 4.56 us -> 2.64 us
    dot_general x6, matrix products: 4.56 us -> 2.64 us  [exact(): lax.dot_general(left, right, (dims, ((), ())), preferred_element_type=jnp...]
where the time goes in v5:
time: 66.5 us; the launch traced here: 66.2 us
  starting transfers between devices  35 us (53%)
  waiting for transfers between devices  15.5 us (23%)
  Pallas kernels  9.57 us (14%)
  matrix products  2.64 us (4%)
  other arithmetic  2.61 us (4%)
  between operations  0.89 us (1%)
    ppermute x4, starting transfers between devices, from_quad(): return lax.ppermute(block, ('z', 'xl', 'xh', 'core'), pairs)  11.9 us
    ppermute x7, starting transfers between devices, near(): return lax.ppermute(block, 'core', [(0, 1), (1, 0)])  6.41 us
    all_to_all x1, starting transfers between devices, shards(): part = lax.all_to_all(part.reshape(8, 8, 512), 'z', 0, 0, tiled=True)  6.36 us
    ppermute x2, waiting for transfers between devices, opposite(): return lax.ppermute(block, 'xh', [(0, 1), (1, 0)])  6 us
    pallas_call x1, Pallas kernels, product(): pl.pallas_call(product_kernel, in_specs=[pl.BlockSpec(memory_space=pltpu....  5.87 us
    all_to_all x1, waiting for transfers between devices, shards(): part = lax.all_to_all(part.reshape(8, 8, 512), 'z', 0, 0, tiled=True)  5.18 us
    all_to_all x1, starting transfers between devices, shards(): part = lax.all_to_all(part, ('xl', 'y'), 0, 0, tiled=True)  4.34 us
    ppermute x1, starting transfers between devices, far(): return lax.ppermute(block, NEAR, [(s, s ^ 6) for s in range(8)])  3.39 us
  transfers between devices with their start and end apart: 16, of which 10 were waited for; matrix products, arithmetic and copies ran while one was open for 3% of the time, Pallas kernels for 6%

profile of v5, /device:TPU:1, one launch (start us, length us, event | category | flops | bytes accessed | tf_op | source)
XLA Modules:
  0.0 66.2 jit_solution(5961649499915731644)
XLA Ops:
  0.7 0.1 pad_add_fusion.at_ref
  0.7 5.9 %product.1 = (f32[512,512]{1,0:T(8,128)S(1)}, f32[256,256]{1,0:T(8,128)S(1)}) custom-call(s32[4]{0:T(128)S(1)} %pad_add_fusion.at_ref, f32[512,2048]{1,0:T(8,128)} %bitcast.40, f32[2048,512]{1,0:T(8,128)} %solved_hbm.1, f32[2,256,1024]{2,1,0:T(8,128)} %inverse_hbm.1), custom_call_target="tpu_custom_call" | custom-call | flops 3221225472 | bytes 9437184 | tf_op jit(solution)/shard_map/product/pallas_call | solution.py:54
  6.6 3.4 %collective-permute-start.1 = (f32[256,256]{1,0:T(8,128)S(1)}, f32[256,256]{1,0:T(8,128)S(1)}, u32[]{:S(2)}, u32[]{:S(2)}) collective-permute-start(f32[256,256]{1,0:T(8,128)S(1)} %get-tuple-element.7.p0), channel_id=1, source_target_pairs={{0,18},{1,19},{2,16},{3,17},{16,2},{17,3},{18,0},{19,1},{4,22},{5,... | collective-permute-start | bytes 786440 | tf_op jit(solution)/shard_map/ppermute | solution.py:168
  10.0 1.8 %place.1 = f32[8,64,512]{2,1,0:T(8,128)} custom-call(s32[4]{0:T(128)S(1)} %pad_add_fusion.at_ref, f32[512,512]{1,0:T(8,128)S(1)} %get-tuple-element.6.update_ref, f32[2,8,256]{2,1,0:T(8,128)S(1)} %bitcast.33), custom_call_target="tpu_custom_call" | custom-call | flops 262144 | bytes 2097152 | tf_op jit(solution)/shard_map/place/pallas_call | solution.py:95
  11.8 0.0 copy-start
  11.8 4.3 %all-to-all-start = ((f32[8,64,512]{2,1,0:T(8,128)}), f32[8,64,512]{2,1,0:T(8,128)S(1)}, u32[]{:S(2)}, u32[]{:S(2)}) async-start(f32[8,64,512]{2,1,0:T(8,128)} %place.1), calls=%async_computation | async-start | bytes 2097152 | tf_op jit(solution)/shard_map/all_to_all | solution.py:216
  16.2 1.2 %collective-permute-start = (f32[256,256]{1,0:T(8,128)S(1)}, f32[256,256]{1,0:T(8,128)S(1)}, u32[]{:S(2)}, u32[]{:S(2)}) collective-permute-start(f32[256,256]{1,0:T(8,128)S(1)} %get-tuple-element.7.p0), channel_id=1, source_target_pairs={{0,1},{1,0},{2,3},{3,2},{4,5},{5,4},{6,7},{7,6},{8,9},{9,8},{10,11... | collective-permute-start | bytes 786440 | tf_op jit(solution)/shard_map/ppermute | solution.py:164
  17.4 0.0 collective-permute-done.1.p2
  17.4 0.2 collective-permute-start.2
  17.6 0.4 collective-permute-start.3
  18.0 0.1 collective-permute-start.4
  18.1 0.4 collective-permute-start.5
  18.5 0.2 collective-permute-done.2
  18.8 0.2 collective-permute-done.3
  18.9 0.4 collective-permute-done.4
  19.3 0.2 collective-permute-done.5
  19.5 0.0 collective-permute-done.p1
  19.5 0.0 copy-done
  19.5 1.2 %middle.1 = f32[256,256]{1,0:T(8,128)S(1)} custom-call(s32[4]{0:T(128)S(1)} %pad_add_fusion.at_ref, f32[256,1024]{1,0:T(8,128)S(1)} %copy-done, f32[256,256]{1,0:T(8,128)S(1)} %get-tuple-element.7.p0, f32[256,256]{1,0:T(8,128)S(1)} %collective-permute-done.p1, f32[256,256]{1,0:T(8,128)S(1)} %collective-permute-done.1.p2, f32[256,256]{1,0:T(8,128)S(1)} %pad_maximum_fusion.p3), custom_call_target="tpu_custom_call" | custom-call | flops 1024 | bytes 1024 | tf_op jit(solution)/shard_map/middle/pallas_call | solution.py:151
  20.7 0.4 collective-permute-start.6
  21.1 7.9 %collective-permute-start.7 = (f32[256,256]{1,0:T(8,128)S(1)}, f32[256,256]{1,0:T(8,128)}, u32[]{:S(2)}, u32[]{:S(2)}) collective-permute-start(f32[256,256]{1,0:T(8,128)S(1)} %middle.1), channel_id=1, source_target_pairs={{18,0},{50,1},{66,2},{226,3},{2,16},{34,17},{82,18},{242,19},{19,3... | collective-permute-start | bytes 786440 | tf_op jit(solution)/shard_map/ppermute | solution.py:189
  29.0 1.5 %collective-permute-start.8 = (f32[256,256]{1,0:T(8,128)S(1)}, f32[256,256]{1,0:T(8,128)}, u32[]{:S(2)}, u32[]{:S(2)}) collective-permute-start(f32[256,256]{1,0:T(8,128)S(1)} %middle.1), channel_id=1, source_target_pairs={{19,0},{51,1},{67,2},{227,3},{3,16},{35,17},{83,18},{243,19},{0,32... | collective-permute-start | bytes 786440 | tf_op jit(solution)/shard_map/ppermute | solution.py:189
  30.5 2.1 %collective-permute-start.9 = (f32[256,256]{1,0:T(8,128)S(1)}, f32[256,256]{1,0:T(8,128)}, u32[]{:S(2)}, u32[]{:S(2)}) collective-permute-start(f32[256,256]{1,0:T(8,128)S(1)} %middle.1), channel_id=1, source_target_pairs={{0,0},{32,1},{80,2},{240,3},{16,16},{48,17},{64,18},{224,19},{1,32... | collective-permute-start | bytes 786440 | tf_op jit(solution)/shard_map/ppermute | solution.py:189
  32.7 0.0 all-to-all-done.parts_ref
  32.7 0.7 %sum_parts.1 = f32[64,512]{1,0:T(8,128)} custom-call(f32[8,64,512]{2,1,0:T(8,128)S(1)} %all-to-all-done.parts_ref), custom_call_target="tpu_custom_call" | custom-call | flops 262144 | bytes 1048576 | tf_op jit(solution)/shard_map/sum_parts/pallas_call | solution.py:116
  33.4 6.4 %all-to-all-start.1 = ((f32[8,8,512]{2,1,0:T(8,128)}), f32[8,8,512]{2,1,0:T(8,128)S(1)}, u32[]{:S(2)}, u32[]{:S(2)}) async-start(f32[8,8,512]{2,1,0:T(8,128)} %bitcast.6), calls=%async_computation.1 | async-start | bytes 262144 | tf_op jit(solution)/shard_map/all_to_all | solution.py:221
  39.7 0.0 collective-permute-done.6
  39.8 0.0 collective-permute-done.7
  39.8 1.6 %collective-permute-done.8 = f32[256,256]{1,0:T(8,128)} collective-permute-done((f32[256,256]{1,0:T(8,128)S(1)}, f32[256,256]{1,0:T(8,128)}, u32[]{:S(2)}, u32[]{:S(2)}) %collective-permute-start.8) | collective-permute-done | bytes 262176 | tf_op jit(solution)/shard_map/ppermute | solution.py:189
  41.4 0.0 collective-permute-done.9
  41.4 1.2 %broadcast_select_fusion.7 = (f32[256,256]{1,0:T(8,128)S(1)}, f32[256,256]{1,0:T(8,128)S(1)}, f32[256,256]{1,0:T(8,128)S(1)}, f32[256,256]{1,0:T(8,128)S(1)}) fusion(pred[]{:T(512)S(6)} %eq.44, f32[256,256]{1,0:T(8,128)S(1)} %collective-permute-done.6, f32[256,256]{1,0:T(8,128)} %collective-permute-done.7, pred[]{:T(512)S(6)} %eq.45, ...), kind=kLoop, calls=%fused_computation.36 | loop fusion | flops 524288 | bytes 2097154 | tf_op jit(solution)/shard_map/jit(_where)/select_n | solution.py:200
  42.6 5.2 %all-to-all-done.1 = f32[8,8,512]{2,1,0:T(8,128)S(1)} async-done(((f32[8,8,512]{2,1,0:T(8,128)}), f32[8,8,512]{2,1,0:T(8,128)S(1)}, u32[]{:S(2)}, u32[]{:S(2)}) %all-to-all-start.1) | async-done | bytes 131104 | tf_op jit(solution)/shard_map/all_to_all | solution.py:221
  47.8 0.5 convolution_subtract_fusion
  48.3 2.5 %collective-permute-start.10 = (f32[8,1280]{1,0:T(8,128)S(1)}, f32[8,1280]{1,0:T(8,128)S(1)}, u32[]{:S(2)}, u32[]{:S(2)}) collective-permute-start(f32[8,1280]{1,0:T(8,128)S(1)} %pad_maximum_fusion.4), channel_id=1, source_target_pairs={{0,1},{1,0},{2,3},{3,2},{4,5},{5,4},{6,7},{7,6},{8,9},{9,8},{10,11... | collective-permute-start | bytes 122888 | tf_op jit(solution)/shard_map/ppermute | solution.py:164
  50.8 0.9 %collective-permute-done.10 = f32[8,1280]{1,0:T(8,128)S(1)} collective-permute-done((f32[8,1280]{1,0:T(8,128)S(1)}, f32[8,1280]{1,0:T(8,128)S(1)}, u32[]{:S(2)}, u32[]{:S(2)}) %collective-permute-start.10) | collective-permute-done | bytes 40992 | tf_op jit(solution)/shard_map/ppermute | solution.py:164
  51.7 1.4 %collective-permute-start.11 = (f32[8,1536]{1,0:T(8,128)S(1)}, f32[8,1536]{1,0:T(8,128)S(1)}, u32[]{:S(2)}, u32[]{:S(2)}) collective-permute-start(f32[8,1536]{1,0:T(8,128)S(1)} %pad_maximum_fusion.3), channel_id=1, source_target_pairs={{0,2},{2,0},{1,3},{3,1},{4,6},{6,4},{5,7},{7,5},{8,10},{10,8},{9,1... | collective-permute-start | bytes 147464 | tf_op jit(solution)/shard_map/ppermute | solution.py:172
  53.1 3.3 %collective-permute-done.11 = f32[8,1536]{1,0:T(8,128)S(1)} collective-permute-done((f32[8,1536]{1,0:T(8,128)S(1)}, f32[8,1536]{1,0:T(8,128)S(1)}, u32[]{:S(2)}, u32[]{:S(2)}) %collective-permute-start.11) | collective-permute-done | bytes 49184 | tf_op jit(solution)/shard_map/ppermute | solution.py:172
  56.4 0.5 fusion.21
  57.0 0.4 fusion.19
  57.3 0.5 fusion.17
  57.8 0.4 fusion.15
  58.2 1.6 %collective-permute-start.12 = (f32[8,1536]{1,0:T(8,128)S(1)}, f32[8,1536]{1,0:T(8,128)S(1)}, u32[]{:S(2)}, u32[]{:S(2)}) collective-permute-start(f32[8,1536]{1,0:T(8,128)S(1)} %fusion.29), channel_id=1, source_target_pairs={{0,1},{1,0},{2,3},{3,2},{4,5},{5,4},{6,7},{7,6},{8,9},{9,8},{10,11... | collective-permute-start | bytes 147464 | tf_op jit(solution)/shard_map/ppermute | solution.py:164
  59.8 0.9 %collective-permute-done.12 = f32[8,1536]{1,0:T(8,128)S(1)} collective-permute-done((f32[8,1536]{1,0:T(8,128)S(1)}, f32[8,1536]{1,0:T(8,128)S(1)}, u32[]{:S(2)}, u32[]{:S(2)}) %collective-permute-start.12) | collective-permute-done | bytes 49184 | tf_op jit(solution)/shard_map/ppermute | solution.py:164
  60.7 1.2 %collective-permute-start.13 = (f32[8,1280]{1,0:T(8,128)S(1)}, f32[8,1280]{1,0:T(8,128)S(1)}, u32[]{:S(2)}, u32[]{:S(2)}) collective-permute-start(f32[8,1280]{1,0:T(8,128)S(1)} %pad_maximum_fusion.5), channel_id=1, source_target_pairs={{0,2},{2,0},{1,3},{3,1},{4,6},{6,4},{5,7},{7,5},{8,10},{10,8},{9,1... | collective-permute-start | bytes 122888 | tf_op jit(solution)/shard_map/ppermute | solution.py:172
  61.9 0.6 maximum_bitcast_fusion
  62.5 2.7 %collective-permute-done.13 = f32[8,1280]{1,0:T(8,128)S(1)} collective-permute-done((f32[8,1280]{1,0:T(8,128)S(1)}, f32[8,1280]{1,0:T(8,128)S(1)}, u32[]{:S(2)}, u32[]{:S(2)}) %collective-permute-start.13) | collective-permute-done | bytes 40992 | tf_op jit(solution)/shard_map/ppermute | solution.py:172
  65.2 0.4 fusion.33
  65.6 0.6 maximum_bitcast_fusion.1
  (22 shorter events, 0.2 us)
Async XLA Ops:
  0.7 9.3 %copy-start.1 = (f32[2,256,8]{1,2,0:T(8,128)S(1)}, f32[2,256,8]{1,2,0:T(8,128)}, u32[]{:S(2)}) copy-start(f32[2,256,8]{1,2,0:T(8,128)} %param.7) | copy-start | bytes 49156
  6.6 10.8 %collective-permute-start.1 = (f32[256,256]{1,0:T(8,128)S(1)}, f32[256,256]{1,0:T(8,128)S(1)}, u32[]{:S(2)}, u32[]{:S(2)}) collective-permute-start(f32[256,256]{1,0:T(8,128)S(1)} %get-tuple-element.7.p0), channel_id=1, source_target_pairs={{0,18},{1,19},{2,16},{3,17},{16,2},{17,3},{18,0},{19,1},{4,22},{5,... | collective-permute-start | bytes 786440 | tf_op jit(solution)/shard_map/ppermute | solution.py:168
  11.8 7.7 %copy-start = (f32[256,1024]{1,0:T(8,128)S(1)}, f32[256,1024]{1,0:T(8,128)}, u32[]{:S(2)}) copy-start(f32[256,1024]{1,0:T(8,128)} %left_ref.1) | copy-start | bytes 3145732
  11.8 20.8 %all-to-all-start = ((f32[8,64,512]{2,1,0:T(8,128)}), f32[8,64,512]{2,1,0:T(8,128)S(1)}, u32[]{:S(2)}, u32[]{:S(2)}) async-start(f32[8,64,512]{2,1,0:T(8,128)} %place.1), calls=%async_computation | async-start | bytes 2097152 | tf_op jit(solution)/shard_map/all_to_all | solution.py:216
  16.2 3.3 %collective-permute-start = (f32[256,256]{1,0:T(8,128)S(1)}, f32[256,256]{1,0:T(8,128)S(1)}, u32[]{:S(2)}, u32[]{:S(2)}) collective-permute-start(f32[256,256]{1,0:T(8,128)S(1)} %get-tuple-element.7.p0), channel_id=1, source_target_pairs={{0,1},{1,0},{2,3},{3,2},{4,5},{5,4},{6,7},{7,6},{8,9},{9,8},{10,11... | collective-permute-start | bytes 786440 | tf_op jit(solution)/shard_map/ppermute | solution.py:164
  17.4 1.3 %collective-permute-start.2 = (f32[64,256]{1,0:T(8,128)S(1)}, f32[64,256]{1,0:T(8,128)S(1)}, u32[]{:S(2)}, u32[]{:S(2)}) collective-permute-start(f32[64,256]{1,0:T(8,128)S(1)} %get-tuple-element.14), channel_id=1, source_target_pairs={{0,1},{1,0},{2,3},{3,2},{4,5},{5,4},{6,7},{7,6},{8,9},{9,8},{10,11... | collective-permute-start | bytes 196616 | tf_op jit(solution)/shard_map/ppermute | solution.py:164
  17.6 1.3 %collective-permute-start.3 = (f32[64,256]{1,0:T(8,128)S(1)}, f32[64,256]{1,0:T(8,128)S(1)}, u32[]{:S(2)}, u32[]{:S(2)}) collective-permute-start(f32[64,256]{1,0:T(8,128)S(1)} %get-tuple-element.17), channel_id=1, source_target_pairs={{0,1},{1,0},{2,3},{3,2},{4,5},{5,4},{6,7},{7,6},{8,9},{9,8},{10,11... | collective-permute-start | bytes 196616 | tf_op jit(solution)/shard_map/ppermute | solution.py:164
  18.0 1.3 %collective-permute-start.4 = (f32[64,256]{1,0:T(8,128)S(1)}, f32[64,256]{1,0:T(8,128)S(1)}, u32[]{:S(2)}, u32[]{:S(2)}) collective-permute-start(f32[64,256]{1,0:T(8,128)S(1)} %get-tuple-element.16), channel_id=1, source_target_pairs={{0,1},{1,0},{2,3},{3,2},{4,5},{5,4},{6,7},{7,6},{8,9},{9,8},{10,11... | collective-permute-start | bytes 196616 | tf_op jit(solution)/shard_map/ppermute | solution.py:164
  18.1 1.3 %collective-permute-start.5 = (f32[64,256]{1,0:T(8,128)S(1)}, f32[64,256]{1,0:T(8,128)S(1)}, u32[]{:S(2)}, u32[]{:S(2)}) collective-permute-start(f32[64,256]{1,0:T(8,128)S(1)} %get-tuple-element.15), channel_id=1, source_target_pairs={{0,1},{1,0},{2,3},{3,2},{4,5},{5,4},{6,7},{7,6},{8,9},{9,8},{10,11... | collective-permute-start | bytes 196616 | tf_op jit(solution)/shard_map/ppermute | solution.py:164
  20.7 19.1 %collective-permute-start.6 = (f32[256,256]{1,0:T(8,128)S(1)}, f32[256,256]{1,0:T(8,128)S(1)}, u32[]{:S(2)}, u32[]{:S(2)}) collective-permute-start(f32[256,256]{1,0:T(8,128)S(1)} %middle.1), channel_id=1, source_target_pairs={{1,0},{33,1},{81,2},{241,3},{17,16},{49,17},{65,18},{225,19},{18,3... | collective-permute-start | bytes 786440 | tf_op jit(solution)/shard_map/ppermute | solution.py:189
  21.1 18.6 %collective-permute-start.7 = (f32[256,256]{1,0:T(8,128)S(1)}, f32[256,256]{1,0:T(8,128)}, u32[]{:S(2)}, u32[]{:S(2)}) collective-permute-start(f32[256,256]{1,0:T(8,128)S(1)} %middle.1), channel_id=1, source_target_pairs={{18,0},{50,1},{66,2},{226,3},{2,16},{34,17},{82,18},{242,19},{19,3... | collective-permute-start | bytes 786440 | tf_op jit(solution)/shard_map/ppermute | solution.py:189
  29.0 12.4 %collective-permute-start.8 = (f32[256,256]{1,0:T(8,128)S(1)}, f32[256,256]{1,0:T(8,128)}, u32[]{:S(2)}, u32[]{:S(2)}) collective-permute-start(f32[256,256]{1,0:T(8,128)S(1)} %middle.1), channel_id=1, source_target_pairs={{19,0},{51,1},{67,2},{227,3},{3,16},{35,17},{83,18},{243,19},{0,32... | collective-permute-start | bytes 786440 | tf_op jit(solution)/shard_map/ppermute | solution.py:189
  30.5 10.9 %collective-permute-start.9 = (f32[256,256]{1,0:T(8,128)S(1)}, f32[256,256]{1,0:T(8,128)}, u32[]{:S(2)}, u32[]{:S(2)}) collective-permute-start(f32[256,256]{1,0:T(8,128)S(1)} %middle.1), channel_id=1, source_target_pairs={{0,0},{32,1},{80,2},{240,3},{16,16},{48,17},{64,18},{224,19},{1,32... | collective-permute-start | bytes 786440 | tf_op jit(solution)/shard_map/ppermute | solution.py:189
  33.4 14.4 %all-to-all-start.1 = ((f32[8,8,512]{2,1,0:T(8,128)}), f32[8,8,512]{2,1,0:T(8,128)S(1)}, u32[]{:S(2)}, u32[]{:S(2)}) async-start(f32[8,8,512]{2,1,0:T(8,128)} %bitcast.6), calls=%async_computation.1 | async-start | bytes 262144 | tf_op jit(solution)/shard_map/all_to_all | solution.py:221
  39.7 16.7 %copy-start.2 = (f32[2,256,1024]{2,1,0:T(8,128)S(1)}, f32[2,256,1024]{2,1,0:T(8,128)}, u32[]{:S(2)}) copy-start(f32[2,256,1024]{2,1,0:T(8,128)} %inverse_hbm.1) | copy-start | bytes 6291460
  48.3 3.4 %collective-permute-start.10 = (f32[8,1280]{1,0:T(8,128)S(1)}, f32[8,1280]{1,0:T(8,128)S(1)}, u32[]{:S(2)}, u32[]{:S(2)}) collective-permute-start(f32[8,1280]{1,0:T(8,128)S(1)} %pad_maximum_fusion.4), channel_id=1, source_target_pairs={{0,1},{1,0},{2,3},{3,2},{4,5},{5,4},{6,7},{7,6},{8,9},{9,8},{10,11... | collective-permute-start | bytes 122888 | tf_op jit(solution)/shard_map/ppermute | solution.py:164
  51.7 4.7 %collective-permute-start.11 = (f32[8,1536]{1,0:T(8,128)S(1)}, f32[8,1536]{1,0:T(8,128)S(1)}, u32[]{:S(2)}, u32[]{:S(2)}) collective-permute-start(f32[8,1536]{1,0:T(8,128)S(1)} %pad_maximum_fusion.3), channel_id=1, source_target_pairs={{0,2},{2,0},{1,3},{3,1},{4,6},{6,4},{5,7},{7,5},{8,10},{10,8},{9,1... | collective-permute-start | bytes 147464 | tf_op jit(solution)/shard_map/ppermute | solution.py:172
  58.2 2.5 %collective-permute-start.12 = (f32[8,1536]{1,0:T(8,128)S(1)}, f32[8,1536]{1,0:T(8,128)S(1)}, u32[]{:S(2)}, u32[]{:S(2)}) collective-permute-start(f32[8,1536]{1,0:T(8,128)S(1)} %fusion.29), channel_id=1, source_target_pairs={{0,1},{1,0},{2,3},{3,2},{4,5},{5,4},{6,7},{7,6},{8,9},{9,8},{10,11... | collective-permute-start | bytes 147464 | tf_op jit(solution)/shard_map/ppermute | solution.py:164
  60.7 4.4 %collective-permute-start.13 = (f32[8,1280]{1,0:T(8,128)S(1)}, f32[8,1280]{1,0:T(8,128)S(1)}, u32[]{:S(2)}, u32[]{:S(2)}) collective-permute-start(f32[8,1280]{1,0:T(8,128)S(1)} %pad_maximum_fusion.5), channel_id=1, source_target_pairs={{0,2},{2,0},{1,3},{3,1},{4,6},{6,4},{5,7},{7,5},{8,10},{10,8},{9,1... | collective-permute-start | bytes 122888 | tf_op jit(solution)/shard_map/ppermute | solution.py:172
